TPU v7x, 32 devices: a whole 2x2x4 slice. The times are simulated.
32 devices in a mesh: gx: 8 (over y, x, core), gy: 4 (over z).
Axes of the slice: x: 2, y: 2, z: 4, core: 2. Of those that a mesh axis runs over, the one named last changes fastest.
Arguments:
- density: float32 [8192, 8192], P('gy', 'gx'), may hold values from -6 to 6
- kernel_rows: float32 [8192], P('gy'), may hold values from 0.1 to 1
- kernel_cols: float32 [8192], P('gx'), may hold values from 0.1 to 1
Outputs:
- spectrum_real: float32 [8192, 8192], P('gy', 'gx')
- spectrum_imag: float32 [8192, 8192], P('gy', 'gx')
All inputs are finite; a program needn't handle non-finite values.
Results may differ from a plain program's by a relative error of at most 0.000071.
Values sent between devices are 32-bit elements; how exact they have to be, the bound alone decides.
A program may use at most 384 MiB of HBM per device.

v0:
```python
import math

import jax
import jax.numpy as jnp
from jax import lax
from jax.sharding import PartitionSpec as P

NR = 8192
NC = 8192


HIGHEST = lax.Precision.HIGHEST
TWO_PI = 2.0 * math.pi


def dft_tables(length):
    positions = jnp.arange(length, dtype=jnp.int32)
    phase = positions[:, None] * positions[None, :] % length
    phase_angle = phase.astype(jnp.float32) * (-TWO_PI / length)
    return (jnp.cos(phase_angle), jnp.sin(phase_angle))


def rotate_by(real_part, imag_part, cosine, sine_part):
    return (real_part * cosine - imag_part * sine_part, real_part * sine_part + imag_part * cosine)


def rotate_phase(real_part, imag_part, phase, total):
    phase_angle = (phase % total).astype(jnp.float32) * (-TWO_PI / total)
    return rotate_by(real_part, imag_part, jnp.cos(phase_angle), jnp.sin(phase_angle))


def split_length(length):
    inner = 1
    for factor in range(1, length + 1):
        if factor * factor > length:
            break
        if length % factor == 0:
            inner = factor
    return (inner, length // inner)


def whole_columns_dft(real_part):
    rows_here, length = real_part.shape
    inner, outer = split_length(length)
    cos_outer, sin_outer = dft_tables(outer)
    shaped_real = real_part.reshape(rows_here, outer, inner)
    first_real = jnp.einsum("rqp,qk->rkp", shaped_real, cos_outer, precision=HIGHEST)
    first_imag = jnp.einsum("rqp,qk->rkp", shaped_real, sin_outer, precision=HIGHEST)
    phase = (
        jnp.arange(outer, dtype=jnp.int32)[:, None] * jnp.arange(inner, dtype=jnp.int32)[None, :]
    )
    first_real, first_imag = rotate_phase(first_real, first_imag, phase[None, :, :], length)
    cos_inner, sin_inner = dft_tables(inner)
    new_real = jnp.einsum("rkp,pj->rjk", first_real, cos_inner, precision=HIGHEST) - jnp.einsum(
        "rkp,pj->rjk", first_imag, sin_inner, precision=HIGHEST
    )
    new_imag = jnp.einsum("rkp,pj->rjk", first_real, sin_inner, precision=HIGHEST) + jnp.einsum(
        "rkp,pj->rjk", first_imag, cos_inner, precision=HIGHEST
    )
    return (new_real.reshape(rows_here, length), new_imag.reshape(rows_here, length))


def whole_rows_dft(real_part, imag_part):
    length, width_here = real_part.shape
    inner, outer = split_length(length)
    cos_outer, sin_outer = dft_tables(outer)
    shaped_real = real_part.reshape(outer, inner, width_here)
    shaped_imag = imag_part.reshape(outer, inner, width_here)
    first_real = jnp.einsum("qpc,qk->kpc", shaped_real, cos_outer, precision=HIGHEST) - jnp.einsum(
        "qpc,qk->kpc", shaped_imag, sin_outer, precision=HIGHEST
    )
    first_imag = jnp.einsum("qpc,qk->kpc", shaped_real, sin_outer, precision=HIGHEST) + jnp.einsum(
        "qpc,qk->kpc", shaped_imag, cos_outer, precision=HIGHEST
    )
    phase = (
        jnp.arange(outer, dtype=jnp.int32)[:, None] * jnp.arange(inner, dtype=jnp.int32)[None, :]
    )
    first_real, first_imag = rotate_phase(first_real, first_imag, phase[:, :, None], length)
    cos_inner, sin_inner = dft_tables(inner)
    new_real = jnp.einsum("kpc,pj->jkc", first_real, cos_inner, precision=HIGHEST) - jnp.einsum(
        "kpc,pj->jkc", first_imag, sin_inner, precision=HIGHEST
    )
    new_imag = jnp.einsum("kpc,pj->jkc", first_real, sin_inner, precision=HIGHEST) + jnp.einsum(
        "kpc,pj->jkc", first_imag, cos_inner, precision=HIGHEST
    )
    return (new_real.reshape(length, width_here), new_imag.reshape(length, width_here))


def pencil_transform(density):
    rows_here, width_here = density.shape
    row_slab = lax.all_to_all(density, "gx", split_axis=0, concat_axis=1, tiled=True)
    real_part, imag_part = whole_columns_dft(row_slab)
    column_slab = (
        lax.all_to_all(
            lax.all_to_all(real_part, "gx", split_axis=1, concat_axis=0, tiled=True),
            "gy",
            split_axis=1,
            concat_axis=0,
            tiled=True,
        ),
        lax.all_to_all(
            lax.all_to_all(imag_part, "gx", split_axis=1, concat_axis=0, tiled=True),
            "gy",
            split_axis=1,
            concat_axis=0,
            tiled=True,
        ),
    )
    real_part, imag_part = whole_rows_dft(column_slab[0], column_slab[1])
    returned = (
        lax.all_to_all(real_part, "gy", split_axis=0, concat_axis=1, tiled=True),
        lax.all_to_all(imag_part, "gy", split_axis=0, concat_axis=1, tiled=True),
    )
    return (returned[0].reshape(rows_here, width_here), returned[1].reshape(rows_here, width_here))


def on_device(density, kernel_rows, kernel_cols):
    real_part, imag_part = pencil_transform(density)
    factor = kernel_rows[:, None] * kernel_cols[None, :] * (1.0 / math.sqrt(NR * NC))
    return (real_part * factor, imag_part * factor)


def solution(mesh):
    return jax.shard_map(
        on_device,
        mesh=mesh,
        in_specs=(P("gy", "gx"), P("gy"), P("gx")),
        out_specs=(P("gy", "gx"), P("gy", "gx")),
        check_vma=False,
    )
```

profile of v0, /device:TPU:0, one launch (start us, length us, event | category | flops | bytes accessed | tf_op | source)
XLA Modules:
  0.0 1266.6 jit_solution(14552342869354555914)
XLA Ops:
  6.0 94.4 %all-to-all-done = f32[8,256,1024]{2,1,0:T(8,128)} async-done(((f32[8,256,1024]{2,1,0:T(8,128)}), f32[8,256,1024]{2,1,0:T(8,128)}, u32[]{:S(2)}, u32[]{:S(2)}) %all-to-all-start) | async-done | bytes 8388640 | tf_op jit(solution)/shard_map/all_to_all | solution.py:91
  118.7 14.5 %fusion.27 = f32[128,256,64]{1,0,2:T(8,128)} fusion(f32[256,128,64]{1,0,2:T(8,128)} %copy.59), kind=kOutput, calls=%fused_computation.35 | convolution fusion | flops 3221454848 | bytes 16777216 | tf_op jit(solution)/shard_map/rqp,qk->rkp/dot_general | solution.py:48
  133.2 14.8 %add_bitcast_fusion.1 = (f32[256,128,64]{0,1,2:T(8,128)}, f32[256,128,64]{0,1,2:T(8,128)}) fusion(f32[128,256,64]{1,0,2:T(8,128)} %fusion.27, f32[128,64]{0,1:T(8,128)S(1)} %get-tuple-element.12, f32[128,64]{0,1:T(8,128)S(1)} %get-tuple-element.13, f32[256,128,64]{1,0,2:T(8,128)S(1)} %copy-done.4), kind=kOutput, calls=%fused_computation.7 | convolution fusion | flops 3234037760 | bytes 33619968 | tf_op jit(solution)/shard_map/rqp,qk->rkp/dot_general | solution.py:47
  165.7 10.1 fusion.44
  175.8 9.8 add_bitcast_fusion
  200.3 9.9 fusion.50
  210.2 12.0 subtract_bitcast_fusion
  231.5 62.9 %all-to-all-done.3 = f32[256,8,1024]{0,2,1:T(8,128)} async-done(((f32[256,8,1024]{0,2,1:T(8,128)}), f32[256,8,1024]{0,2,1:T(8,128)}, u32[]{:S(2)}, u32[]{:S(2)}) %all-to-all-start.3) | async-done | bytes 8388640 | tf_op jit(solution)/shard_map/all_to_all | solution.py:102
  299.6 11.6 copy.70
  320.5 73.2 %all-to-all-done.1 = f32[256,8,1024]{0,2,1:T(8,128)} async-done(((f32[256,8,1024]{0,2,1:T(8,128)}), f32[256,8,1024]{0,2,1:T(8,128)}, u32[]{:S(2)}, u32[]{:S(2)}) %all-to-all-start.1) | async-done | bytes 8388640 | tf_op jit(solution)/shard_map/all_to_all | solution.py:95
  399.3 11.6 copy.64
  420.2 160.2 %all-to-all-done.4 = f32[2048,4,256]{0,2,1:T(8,128)} async-done(((f32[2048,4,256]{0,2,1:T(8,128)}), f32[2048,4,256]{0,2,1:T(8,128)}, u32[]{:S(2)}, u32[]{:S(2)}) %all-to-all-start.4) | async-done | bytes 8388640 | tf_op jit(solution)/shard_map/all_to_all | solution.py:101
  594.9 17.5 %fusion.8 = f32[128,64,256]{2,0,1:T(8,128)} fusion(f32[128,64,256]{2,1,0:T(8,128)} %bitcast.73), kind=kOutput, calls=%fused_computation.17 | convolution fusion | flops 3221454848 | bytes 16777216 | tf_op jit(solution)/shard_map/qpc,qk->kpc/dot_general | solution.py:72
  612.5 13.2 %fusion.10 = f32[128,64,256]{2,0,1:T(8,128)} fusion(f32[128,64,256]{2,1,0:T(8,128)S(1)} %bitcast.74), kind=kOutput, calls=%fused_computation.19 | convolution fusion | flops 3221454848 | bytes 16777216 | tf_op jit(solution)/shard_map/qpc,qk->kpc/dot_general | solution.py:69
  625.7 143.0 %all-to-all-done.2 = f32[2048,4,256]{0,2,1:T(8,128)} async-done(((f32[2048,4,256]{0,2,1:T(8,128)}), f32[2048,4,256]{0,2,1:T(8,128)}, u32[]{:S(2)}, u32[]{:S(2)}) %all-to-all-start.2) | async-done | bytes 8388640 | tf_op jit(solution)/shard_map/all_to_all | solution.py:94
  777.4 17.8 %fusion.14 = f32[128,64,256]{2,0,1:T(8,128)} fusion(f32[128,64,256]{2,1,0:T(8,128)} %bitcast.75), kind=kOutput, calls=%fused_computation.23 | convolution fusion | flops 3221454848 | bytes 16777216 | tf_op jit(solution)/shard_map/qpc,qk->kpc/dot_general | solution.py:69
  795.2 20.2 %multiply_subtract_fusion = (f32[128,64,256]{2,0,1:T(8,128)S(1)}, f32[128,64,256]{2,0,1:T(8,128)S(1)}) fusion(f32[128,64]{0,1:T(8,128)S(1)} %get-tuple-element.12, f32[128,64]{0,1:T(8,128)S(1)} %get-tuple-element.13, f32[128,64,256]{2,0,1:T(8,128)} %fusion.8, f32[128,64,256]{2,0,1:T(8,128)} %fusion.14, f32[128,64,256]{2,0,1:T(8,128)} %fusion.10, ...), kind=kOutput, calls=%fused_computation.4 | convolution fusion | flops 3238232064 | bytes 50397184 | tf_op jit(solution)/shard_map/qpc,qk->kpc/dot_general | solution.py:72
  815.4 13.4 %fusion.2 = f32[64,128,256]{2,0,1:T(8,128)} fusion(f32[128,64,256]{2,0,1:T(8,128)S(1)} %get-tuple-element.7), kind=kOutput, calls=%fused_computation.11 | convolution fusion | flops 1610670080 | bytes 16777216 | tf_op jit(solution)/shard_map/kpc,pj->jkc/dot_general | solution.py:80
  828.8 14.5 %fusion.16 = f32[64,128,256]{2,0,1:T(8,128)S(1)} fusion(f32[64,128,256]{2,0,1:T(8,128)} %fusion.2, f32[128,64,256]{2,0,1:T(8,128)S(1)} %get-tuple-element.6), kind=kOutput, calls=%fused_computation.25 | convolution fusion | flops 1612767232 | bytes 25165824 | tf_op jit(solution)/shard_map/kpc,pj->jkc/dot_general | solution.py:80
  857.0 15.8 %fusion = f32[64,128,256]{2,0,1:T(8,128)S(1)} fusion(f32[128,64,256]{2,0,1:T(8,128)} %copy-done.3), kind=kOutput, calls=%fused_computation.9 | convolution fusion | flops 1610670080 | bytes 16777216 | tf_op jit(solution)/shard_map/kpc,pj->jkc/dot_general | solution.py:83
  872.8 16.3 %fusion.19 = f32[64,128,256]{2,0,1:T(8,128)S(1)} fusion(f32[64,128,256]{2,0,1:T(8,128)S(1)} %fusion, f32[128,64,256]{2,0,1:T(8,128)} %copy-done.1), kind=kOutput, calls=%fused_computation.26 | convolution fusion | flops 1612767232 | bytes 25165824 | tf_op jit(solution)/shard_map/kpc,pj->jkc/dot_general | solution.py:83
  897.4 142.2 %all-to-all-done.5 = f32[4,2048,256]{2,1,0:T(8,128)} async-done(((f32[4,2048,256]{2,1,0:T(8,128)}), f32[4,2048,256]{2,1,0:T(8,128)}, u32[]{:S(2)}, u32[]{:S(2)}) %all-to-all-start.5) | async-done | bytes 8388640 | tf_op jit(solution)/shard_map/all_to_all | solution.py:111
  1054.1 173.9 %all-to-all-done.6 = f32[4,2048,256]{2,1,0:T(8,128)} async-done(((f32[4,2048,256]{2,1,0:T(8,128)}), f32[4,2048,256]{2,1,0:T(8,128)}, u32[]{:S(2)}, u32[]{:S(2)}) %all-to-all-start.6) | async-done | bytes 8388640 | tf_op jit(solution)/shard_map/all_to_all | solution.py:112
  1236.7 11.2 bitcast_multiply_fusion
  (38 shorter events, 181.6 us)
Async XLA Ops:
  0.6 99.8 %all-to-all-start = ((f32[8,256,1024]{2,1,0:T(8,128)}), f32[8,256,1024]{2,1,0:T(8,128)}, u32[]{:S(2)}, u32[]{:S(2)}) async-start(f32[8,256,1024]{2,1,0:T(8,128)} %bitcast.82), calls=%async_computation | async-start | bytes 16777216 | tf_op jit(solution)/shard_map/all_to_all | solution.py:91
  118.7 14.5 %copy-start.4 = (f32[256,128,64]{1,0,2:T(8,128)S(1)}, f32[256,128,64]{1,0,2:T(8,128)}, u32[]{:S(2)}) copy-start(f32[256,128,64]{1,0,2:T(8,128)} %copy.59) | copy-start | bytes 25165828
  165.7 10.1 copy-start
  194.8 99.6 %all-to-all-start.3 = ((f32[256,8,1024]{0,2,1:T(8,128)}), f32[256,8,1024]{0,2,1:T(8,128)}, u32[]{:S(2)}, u32[]{:S(2)}) async-start(f32[256,8,1024]{0,2,1:T(8,128)} %bitcast.78), calls=%async_computation.3 | async-start | bytes 16777216 | tf_op jit(solution)/shard_map/all_to_all | solution.py:102
  294.4 99.3 %all-to-all-start.1 = ((f32[256,8,1024]{0,2,1:T(8,128)}), f32[256,8,1024]{0,2,1:T(8,128)}, u32[]{:S(2)}, u32[]{:S(2)}) async-start(f32[256,8,1024]{0,2,1:T(8,128)} %bitcast.77), calls=%async_computation.1 | async-start | bytes 16777216 | tf_op jit(solution)/shard_map/all_to_all | solution.py:95
  393.7 186.7 %all-to-all-start.4 = ((f32[2048,4,256]{0,2,1:T(8,128)}), f32[2048,4,256]{0,2,1:T(8,128)}, u32[]{:S(2)}, u32[]{:S(2)}) async-start(f32[2048,4,256]{0,2,1:T(8,128)} %all_to_all.100), calls=%async_computation.4 | async-start | bytes 16777216 | tf_op jit(solution)/shard_map/all_to_all | solution.py:101
  580.4 188.3 %all-to-all-start.2 = ((f32[2048,4,256]{0,2,1:T(8,128)}), f32[2048,4,256]{0,2,1:T(8,128)}, u32[]{:S(2)}, u32[]{:S(2)}) async-start(f32[2048,4,256]{0,2,1:T(8,128)} %all_to_all.94), calls=%async_computation.2 | async-start | bytes 16777216 | tf_op jit(solution)/shard_map/all_to_all | solution.py:94
  594.9 17.5 %copy-start.2 = (f32[4,2048,256]{2,1,0:T(8,128)S(1)}, f32[4,2048,256]{2,1,0:T(8,128)}, u32[]{:S(2)}) copy-start(f32[4,2048,256]{2,1,0:T(8,128)} %copy.71) | copy-start | bytes 25165828
  815.4 13.4 %copy-start.3 = (f32[128,64,256]{2,0,1:T(8,128)}, f32[128,64,256]{2,0,1:T(8,128)S(1)}, u32[]{:S(2)}) copy-start(f32[128,64,256]{2,0,1:T(8,128)S(1)} %get-tuple-element.7) | copy-start | bytes 25165828
  815.4 13.4 %copy-start.1 = (f32[128,64,256]{2,0,1:T(8,128)}, f32[128,64,256]{2,0,1:T(8,128)S(1)}, u32[]{:S(2)}) copy-start(f32[128,64,256]{2,0,1:T(8,128)S(1)} %get-tuple-element.6) | copy-start | bytes 25165828
  851.4 188.2 %all-to-all-start.5 = ((f32[4,2048,256]{2,1,0:T(8,128)}), f32[4,2048,256]{2,1,0:T(8,128)}, u32[]{:S(2)}, u32[]{:S(2)}) async-start(f32[4,2048,256]{2,1,0:T(8,128)} %bitcast.79), calls=%async_computation.5 | async-start | bytes 16777216 | tf_op jit(solution)/shard_map/all_to_all | solution.py:111
  1039.6 188.4 %all-to-all-start.6 = ((f32[4,2048,256]{2,1,0:T(8,128)}), f32[4,2048,256]{2,1,0:T(8,128)}, u32[]{:S(2)}, u32[]{:S(2)}) async-start(f32[4,2048,256]{2,1,0:T(8,128)} %bitcast.80), calls=%async_computation.6 | async-start | bytes 16777216 | tf_op jit(solution)/shard_map/all_to_all | solution.py:112
  1228.0 8.7 copy-start.5
  1228.0 8.7 copy-start.6
where the time goes:
time: 1280 us; the launch traced here: 1270 us
  waiting for transfers between devices  850 us (66%)
  matrix products  200 us (16%)
  local copies, waits for them, and re-layouts  166 us (13%)
  starting transfers between devices  38.9 us (3%)
    all_to_all x1, waiting for transfers between devices, pencil_transform(): lax.all_to_all(imag_part, 'gy', split_axis=0, concat_axis=1, tiled=True)  174 us
    all_to_all x1, waiting for transfers between devices, pencil_transform(): lax.all_to_all(lax.all_to_all(imag_part, 'gx', split_axis=1, concat_axis=...  160 us
    all_to_all x1, waiting for transfers between devices, pencil_transform(): lax.all_to_all(lax.all_to_all(real_part, 'gx', split_axis=1, concat_axis=...  143 us
    all_to_all x1, waiting for transfers between devices, pencil_transform(): lax.all_to_all(real_part, 'gy', split_axis=0, concat_axis=1, tiled=True)  142 us
    all_to_all x1, waiting for transfers between devices, pencil_transform(): lax.all_to_all(density, 'gx', split_axis=0, concat_axis=1, tiled=True)  94.4 us
    all_to_all x1, waiting for transfers between devices, pencil_transform(): lax.all_to_all(real_part, 'gx', split_axis=1, concat_axis=0, tiled=True)  73.2 us
    all_to_all x1, waiting for transfers between devices, pencil_transform(): lax.all_to_all(imag_part, 'gx', split_axis=1, concat_axis=0, tiled=True)  62.9 us
  transfers between devices with their start and end apart: 7, of which 7 were waited for; matrix products, arithmetic and copies ran while one was open for 11% of the time, Pallas kernels for 0%

commit v1 on v0

--- a/solution.py
+++ b/solution.py
@@ -3,6 +3,8 @@
 import jax
 import jax.numpy as jnp
 from jax import lax
+from jax.experimental import pallas as pl
+from jax.experimental.pallas import tpu as pltpu
 from jax.sharding import PartitionSpec as P
 
 NR = 8192
@@ -120,9 +122,302 @@
     return (real_part * factor, imag_part * factor)
 
 
+RADIX = 32
+VMEM = pltpu.VMEM
+FULL = pl.BlockSpec(memory_space=pltpu.VMEM)
+
+
+def unit_angle(index, total):
+    angle = (index % total).astype(jnp.float32) * (-TWO_PI / total)
+    return (jnp.cos(angle), jnp.sin(angle))
+
+
+def halves(table):
+    high = lax.reduce_precision(table, exponent_bits=8, mantissa_bits=7)
+    return (high.astype(jnp.bfloat16), (table - high).astype(jnp.bfloat16))
+
+
+def times_root(value, index, total):
+    real, imag = value
+    index = index % total
+    if index == 0:
+        return value
+    if 4 * index == total:
+        return (imag, -real) if imag is not None else (None, -real)
+    if 2 * index == total:
+        return (-real, None if imag is None else -imag)
+    cosine = math.cos(TWO_PI * index / total)
+    sine = -math.sin(TWO_PI * index / total)
+    if imag is None:
+        return (real * cosine, real * sine)
+    if real is None:
+        return (imag * -sine, imag * cosine)
+    return (real * cosine - imag * sine, real * sine + imag * cosine)
+
+
+def plus(left, right):
+    if left is None:
+        return right
+    return left if right is None else left + right
+
+
+def minus(left, right):
+    if right is None:
+        return left
+    return -right if left is None else left - right
+
+
+def small_dft(values, needed):
+    length = len(values)
+    if length == 1:
+        return values
+    half = length // 2
+    keep = min(needed, half)
+    even = small_dft(values[0::2], keep)
+    odd = small_dft(values[1::2], keep)
+    out = [None] * length
+    for k in range(keep):
+        turned = times_root(odd[k], k, length)
+        out[k] = (plus(even[k][0], turned[0]), plus(even[k][1], turned[1]))
+        out[k + half] = (minus(even[k][0], turned[0]), minus(even[k][1], turned[1]))
+    return out
+
+
+def real_dft(values):
+    length = len(values)
+    if length == 1:
+        return [(values[0], None)]
+    half = length // 2
+    even = real_dft(values[0::2])
+    odd = real_dft(values[1::2])
+    out = [None] * (half + 1)
+
+    def entry(spectrum, k):
+        if k < len(spectrum):
+            return spectrum[k]
+        real, imag = spectrum[half - k]
+        return (real, None if imag is None else -imag)
+
+    for k in range(half + 1):
+        if k == half:
+            e, o = even[0], odd[0]
+            out[k] = (minus(e[0], o[0]), None)
+        else:
+            turned = times_root(entry(odd, k), k, length)
+            e = entry(even, k)
+            out[k] = (plus(e[0], turned[0]), plus(e[1], turned[1]))
+    return out
+
+
+def product(left_high, left_low, right_high, right_low):
+    dot = lambda a, b: jnp.dot(a, b, preferred_element_type=jnp.float32)
+    return dot(left_high, right_high) + dot(left_high, right_low) + dot(left_low, right_high)
+
+
+def split_store(high_ref, low_ref, place, value):
+    high = value.astype(jnp.bfloat16)
+    high_ref[place] = high
+    low_ref[place] = (value - high.astype(jnp.float32)).astype(jnp.bfloat16)
+
+
+def rows_kernel(flag, own, near, end, far, cosine, sine, table_high, table_low, kept, sent, high, low):
+    depth = cosine.shape[1]
+    width = own.shape[1]
+    per_block = own.shape[0] // depth
+    count = RADIX // 2 + 1
+    quarter = table_high.shape[0] // 8
+    upper = flag[0] > 0
+
+    @pl.loop(0, depth // 16)
+    def _(step):
+        start = pl.multiple_of(step * 16, 16)
+        for lane in range(0, width, 128):
+            lanes = pl.ds(lane, 128)
+
+            def take(ref, q):
+                return ref[pl.ds(pl.multiple_of(q * depth + start, 16), 16), lanes]
+
+            blocks = []
+            for first, second in ((end, far), (own, near), (near, own), (far, end)):
+                for q in range(per_block):
+                    blocks.append(jnp.where(upper, take(second, q), take(first, q)))
+            spectrum = real_dft(blocks)
+            for k in range(count):
+                real, imag = spectrum[k]
+                if k:
+                    c = cosine[k, pl.ds(start, 16), :]
+                    s = sine[k, pl.ds(start, 16), :]
+                    if imag is None:
+                        real, imag = real * c, real * s
+                    else:
+                        real, imag = real * c - imag * s, real * s + imag * c
+                if imag is None:
+                    imag = jnp.zeros_like(real)
+                split_store(high, low, (k, pl.ds(start, 16), lanes), real)
+                split_store(high, low, (k, pl.ds(pl.multiple_of(depth + start, 16), 16), lanes), imag)
+
+    def put(k, result):
+        rows = pl.ds(pl.multiple_of(k * quarter, 8), quarter)
+        kept[0, rows, :] = result[0:quarter]
+        kept[1, rows, :] = result[quarter : 2 * quarter]
+        sent[0, rows, :] = result[2 * quarter : 3 * quarter]
+        sent[1, rows, :] = result[3 * quarter : 4 * quarter]
+
+    direct = pl.ds(0, 4 * quarter)
+    for k in (0, RADIX // 2):
+        put(k, product(table_high[direct, :], table_low[direct, :], high[k], low[k]))
+
+    @pl.loop(1, RADIX // 2)
+    def _(k):
+        result = product(table_high[...], table_low[...], high[k], low[k])
+        put(k, result[: 4 * quarter])
+        put(RADIX - k, result[4 * quarter :])
+
+
+def rows_stage(flag, own, near, end, far, tables):
+    length, width = own.shape
+    depth = tables[0].shape[1]
+    shape = jax.ShapeDtypeStruct((2, length, width), jnp.float32)
+    count = RADIX // 2 + 1
+    return pl.pallas_call(
+        rows_kernel,
+        out_shape=(shape, shape),
+        in_specs=[pl.BlockSpec(memory_space=pltpu.SMEM)] + [FULL] * 8,
+        out_specs=(FULL, FULL),
+        scratch_shapes=[
+            VMEM((count, 2 * depth, width), jnp.bfloat16),
+            VMEM((count, 2 * depth, width), jnp.bfloat16),
+        ],
+        compiler_params=pltpu.CompilerParams(vmem_limit_bytes=56 * 2**20),
+        cost_estimate=pl.CostEstimate(
+            flops=30 * 10**9, bytes_accessed=24 * 2**20, transcendentals=0
+        ),
+    )(flag, own, near, end, far, *tables)
+
+
+def rows_tables(place, length, blocks):
+    depth = length // RADIX
+    per_block = depth // blocks
+    p = jnp.arange(depth, dtype=jnp.int32)
+    k = jnp.arange(RADIX // 2 + 1, dtype=jnp.int32)
+    cosine, sine = unit_angle(k[:, None] * p[None, :], length)
+    spread = lambda t: jnp.broadcast_to(t[:, :, None], t.shape + (128,))
+    kept = place * per_block + jnp.arange(per_block, dtype=jnp.int32)
+    other = jnp.where(place >= blocks // 2, blocks - 1, 0) * per_block + jnp.arange(
+        per_block, dtype=jnp.int32
+    )
+    parts = []
+    for shift in (0, 1):
+        for which in (kept, other):
+            c, s = unit_angle((which[:, None] + shift) * p[None, :], depth)
+            sign = -1.0 if shift else 1.0
+            parts.append(jnp.concatenate([c, -s * sign], axis=1))
+            parts.append(jnp.concatenate([s, c * sign], axis=1))
+    return (spread(cosine), spread(sine)) + halves(jnp.concatenate(parts, axis=0))
+
+
+def columns_kernel(*refs):
+    parts = refs[:4]
+    cosine, sine, table_high, table_low, out, high, low = refs[4:]
+    groups, _, rows, depth = parts[0].shape
+
+    @pl.loop(0, rows // 16)
+    def _(step):
+        here = pl.ds(pl.multiple_of(step * 16, 16), 16)
+        for lane in range(0, depth, 128):
+            lanes = pl.ds(lane, 128)
+            values = [
+                (parts[q % 4][q // 4, 0, here, lanes], parts[q % 4][q // 4, 1, here, lanes])
+                for q in range(RADIX)
+            ]
+            spectrum = small_dft(values, RADIX)
+            for k in range(RADIX):
+                real, imag = spectrum[k]
+                if k:
+                    c = cosine[pl.ds(k, 1), lanes]
+                    s = sine[pl.ds(k, 1), lanes]
+                    real, imag = real * c - imag * s, real * s + imag * c
+                split_store(high, low, (k, here, lanes), real)
+                split_store(high, low, (k, here, pl.ds(depth + lane, 128)), imag)
+
+    @pl.loop(0, RADIX)
+    def _(k):
+        result = product(high[k], low[k], table_high[...], table_low[...])
+        out[0, k] = result[:, :depth]
+        out[1, k] = result[:, depth:]
+
+
+def columns_stage(parts, length):
+    groups, _, rows, depth = parts[0].shape
+    p = jnp.arange(depth, dtype=jnp.int32)
+    k = jnp.arange(RADIX, dtype=jnp.int32)
+    cosine, sine = unit_angle(k[:, None] * p[None, :], length)
+    c, s = unit_angle(p[:, None] * p[None, :], depth)
+    table = jnp.concatenate(
+        [jnp.concatenate([c, s], axis=1), jnp.concatenate([-s, c], axis=1)], axis=0
+    )
+    tile = 64
+    return pl.pallas_call(
+        columns_kernel,
+        grid=(rows // tile,),
+        out_shape=jax.ShapeDtypeStruct((2, RADIX, rows, depth), jnp.float32),
+        in_specs=[pl.BlockSpec((groups, 2, tile, depth), lambda i: (0, 0, i, 0))] * 4 + [FULL] * 4,
+        out_specs=pl.BlockSpec((2, RADIX, tile, depth), lambda i: (0, 0, i, 0)),
+        scratch_shapes=[
+            VMEM((RADIX, tile, 2 * depth), jnp.bfloat16),
+            VMEM((RADIX, tile, 2 * depth), jnp.bfloat16),
+        ],
+        compiler_params=pltpu.CompilerParams(vmem_limit_bytes=56 * 2**20),
+        cost_estimate=pl.CostEstimate(
+            flops=30 * 10**9, bytes_accessed=32 * 2**20, transcendentals=0
+        ),
+    )(*parts, cosine, sine, *halves(table))
+
+
+def line_transform(density, kernel_rows, kernel_cols, blocks, groups):
+    rows_here, width = density.shape
+    length = rows_here * blocks
+    columns = width * groups
+    place = lax.axis_index("gy")
+    upper = place >= 2
+    inner = (place == 1) | (place == 2)
+    flag = upper.astype(jnp.int32).reshape(1)
+    tables = rows_tables(place, length, blocks)
+    chunk = columns // RADIX
+    parts = []
+    for m in range(width // chunk):
+        own = density[:, m * chunk : (m + 1) * chunk]
+        end = lax.ppermute(own, "gy", [(0, 1), (3, 2)])
+        near = lax.ppermute(own, "gy", [(1, 2), (2, 1)])
+        far = lax.ppermute(own, "gy", [(0, 2), (3, 1)])
+        kept, sent = rows_stage(flag, own, near, end, far, tables)
+        given = lax.ppermute(sent, "gy", [(1, 0), (2, 3)])
+        mine = jnp.where(inner, kept, given)
+        mine = mine.reshape(2, groups, rows_here // groups, chunk).transpose(1, 0, 2, 3)
+        parts.append(lax.all_to_all(mine, "gx", split_axis=0, concat_axis=0, tiled=True))
+    result = columns_stage(parts, columns)
+    rows_part = rows_here // groups
+    share = chunk // groups
+    result = result.reshape(2, RADIX, rows_part, groups, share).transpose(3, 0, 2, 4, 1)
+    result = result.reshape(groups, 2, rows_part, width)
+    result = lax.all_to_all(result, "gx", split_axis=0, concat_axis=0, tiled=True)
+    result = result.transpose(1, 0, 2, 3).reshape(2, RADIX, rows_here // RADIX, width)
+    result = result.transpose(0, 2, 1, 3).reshape(2, rows_here, width)
+    factor = kernel_rows[:, None] * kernel_cols[None, :] * (1.0 / math.sqrt(length * columns))
+    return (result[0] * factor, result[1] * factor)
+
+
 def solution(mesh):
+    blocks, groups = mesh.shape["gy"], mesh.shape["gx"]
+
+    def body(density, kernel_rows, kernel_cols):
+        width = density.shape[1]
+        if blocks == 4 and width % 4 == 0 and 4 * groups == RADIX:
+            return line_transform(density, kernel_rows, kernel_cols, blocks, groups)
+        return on_device(density, kernel_rows, kernel_cols)
+
     return jax.shard_map(
-        on_device,
+        body,
         mesh=mesh,
         in_specs=(P("gy", "gx"), P("gy"), P("gx")),
         out_specs=(P("gy", "gx"), P("gy", "gx")),

time: 1280 us -> 889 us (0.69)
  waiting for transfers between devices: 850 us -> 281 us
  matrix products: 200 us -> 0 us
  blocking collectives: 0 us -> 188 us
  Pallas kernels: 0 us -> 159 us
  starting transfers between devices: 38.9 us -> 139 us
  local copies, waits for them, and re-layouts: 166 us -> 94.3 us
  other arithmetic: 11.3 us -> 25.4 us
    all_to_all x7 -> x4, waiting for transfers between devices: 850 us -> 45.2 us  [line_transform(): lax.all_to_all(mine, 'gx', split_axis=0, concat_axis=0, tiled=True)]
    ppermute x0 -> x16, waiting for transfers between devices: none -> 236 us  [the longest x4 138 us: line_transform(): far = lax.ppermute(own, 'gy', [(0, 2), (3, 1)])]
    dot_general x14 -> x0, matrix products: 200 us -> none  [the longest x1 20.2 us: whole_rows_dft(): jnp.einsum('qpc,qk->kpc', shaped_real, sin_outer, precision=HIGHEST)]
    all_to_all x0 -> x1, blocking collectives: none -> 188 us  [line_transform(): lax.all_to_all(result, 'gx', split_axis=0, concat_axis=0, tiled=True)]
    pallas_call x0 -> x5, Pallas kernels: none -> 159 us  [the longest x4 95.5 us: rows_stage(): pl.pallas_call(rows_kernel, out_shape=(shape, shape), in_specs=[pl.BlockS...]
    ppermute x0 -> x16, starting transfers between devices: none -> 121 us  [the longest x4 57.4 us: line_transform(): end = lax.ppermute(own, 'gy', [(0, 1), (3, 2)])]
    all_to_all x11 -> x0, local copies, waits for them, and re-layouts: 104 us -> none  [the longest x2 20.9 us: pencil_transform(): lax.all_to_all(real_part, 'gx', split_axis=1, concat_axis=0, tiled=True)]
    transpose x0 -> x2, local copies, waits for them, and re-layouts: none -> 32.9 us  [the longest x1 17.7 us: line_transform(): result.transpose(1, 0, 2, 3).reshape(2, RADIX, rows_here // RADIX, width)]
  transfers between devices with their start and end apart: 7 -> 20, of which waited for: 7 -> 10; matrix products, arithmetic and copies ran while one was open for 11% -> 4% of each run, Pallas kernels for 0% -> 11%
where the time goes in v1:
time: 889 us; the launch traced here: 888 us
  waiting for transfers between devices  281 us (32%)
  blocking collectives  188 us (21%)
  Pallas kernels  159 us (18%)
  starting transfers between devices  139 us (16%)
  local copies, waits for them, and re-layouts  94.3 us (11%)
  other arithmetic  25.4 us (3%)
    all_to_all x1, blocking collectives, line_transform(): lax.all_to_all(result, 'gx', split_axis=0, concat_axis=0, tiled=True)  188 us
    ppermute x4, waiting for transfers between devices, line_transform(): far = lax.ppermute(own, 'gy', [(0, 2), (3, 1)])  138 us
    ppermute x4, waiting for transfers between devices, line_transform(): given = lax.ppermute(sent, 'gy', [(1, 0), (2, 3)])  96.4 us
    pallas_call x4, Pallas kernels, rows_stage(): pl.pallas_call(rows_kernel, out_shape=(shape, shape), in_specs=[pl.BlockS...  95.5 us
    pallas_call x1, Pallas kernels, columns_stage(): pl.pallas_call(columns_kernel, grid=(rows // tile,), out_shape=jax.ShapeD...  63.7 us
    ppermute x4, starting transfers between devices, line_transform(): end = lax.ppermute(own, 'gy', [(0, 1), (3, 2)])  57.4 us
    ppermute x4, starting transfers between devices, line_transform(): far = lax.ppermute(own, 'gy', [(0, 2), (3, 1)])  50.3 us
    all_to_all x4, waiting for transfers between devices, line_transform(): lax.all_to_all(mine, 'gx', split_axis=0, concat_axis=0, tiled=True)  45.2 us
  transfers between devices with their start and end apart: 20, of which 10 were waited for; matrix products, arithmetic and copies ran while one was open for 4% of the time, Pallas kernels for 11%

profile of v1, /device:TPU:0, one launch (start us, length us, event | category | flops | bytes accessed | tf_op | source)
XLA Modules:
  0.0 887.9 jit_solution(75084036989329500)
XLA Ops:
  8.9 7.8 collective-permute-start.13
  27.0 35.7 %collective-permute-start.9 = (f32[2048,256]{1,0:T(8,128)}, f32[2048,256]{1,0:T(8,128)S(1)}, u32[]{:S(2)}, u32[]{:S(2)}) collective-permute-start(f32[2048,256]{1,0:T(8,128)} %get-tuple-element.23.own), channel_id=1, source_target_pairs={{0,1},{3,2},{4,5},{7,6},{8,9},{11,10},{12,13},{15,14},{16,17},{19,... | collective-permute-start | bytes 6291464 | tf_op jit(solution)/shard_map/ppermute | solution.py:390
  62.7 44.0 %collective-permute-done.14.far = f32[2048,256]{1,0:T(8,128)} collective-permute-done((f32[2048,256]{1,0:T(8,128)}, f32[2048,256]{1,0:T(8,128)}, u32[]{:S(2)}, u32[]{:S(2)}) %collective-permute-start.14) | collective-permute-done | bytes 2097184 | tf_op jit(solution)/shard_map/ppermute | solution.py:392
  110.9 23.9 %shard_map.53 = (f32[2,2048,256]{2,1,0:T(8,128)}, f32[2,2048,256]{2,1,0:T(8,128)}) custom-call(s32[1]{0:T(128)} %bitcast.flag, f32[2048,256]{1,0:T(8,128)} %get-tuple-element.20.own, f32[2048,256]{1,0:T(8,128)} %collective-permute-done.12.near, f32[2048,256]{1,0:T(8,128)} %collective-permute-done.13.end, f32[2048,256]{1,0:T(8,128)} %collective-permute-done.14.far, ...), custom_call_target="tpu_custom_call" | custom-call | flops 30000001024 | bytes 25165824 | tf_op jit(solution)/shard_map/pallas_call | solution.py:282
  138.1 13.6 %collective-permute-done.10.far = f32[2048,256]{1,0:T(8,128)} collective-permute-done((f32[2048,256]{1,0:T(8,128)}, f32[2048,256]{1,0:T(8,128)}, u32[]{:S(2)}, u32[]{:S(2)}) %collective-permute-start.10) | collective-permute-done | bytes 2097184 | tf_op jit(solution)/shard_map/ppermute | solution.py:392
  157.3 42.5 %collective-permute-start.6 = (f32[2048,256]{1,0:T(8,128)}, f32[2048,256]{1,0:T(8,128)}, u32[]{:S(2)}, u32[]{:S(2)}) collective-permute-start(f32[2048,256]{1,0:T(8,128)} %get-tuple-element.21.own), channel_id=1, source_target_pairs={{0,2},{3,1},{4,6},{7,5},{8,10},{11,9},{12,14},{15,13},{16,18},{19,... | collective-permute-start | bytes 6291464 | tf_op jit(solution)/shard_map/ppermute | solution.py:392
  201.1 23.9 %shard_map.52 = (f32[2,2048,256]{2,1,0:T(8,128)}, f32[2,2048,256]{2,1,0:T(8,128)}) custom-call(s32[1]{0:T(128)} %bitcast.flag, f32[2048,256]{1,0:T(8,128)} %get-tuple-element.23.own, f32[2048,256]{1,0:T(8,128)} %collective-permute-done.8.near, f32[2048,256]{1,0:T(8,128)} %copy-done.5, f32[2048,256]{1,0:T(8,128)} %collective-permute-done.10.far, ...), custom_call_target="tpu_custom_call" | custom-call | flops 30000001024 | bytes 25165824 | tf_op jit(solution)/shard_map/pallas_call | solution.py:282
  238.4 8.2 collective-permute-start.1
  249.2 37.4 %collective-permute-done.6.far = f32[2048,256]{1,0:T(8,128)} collective-permute-done((f32[2048,256]{1,0:T(8,128)}, f32[2048,256]{1,0:T(8,128)}, u32[]{:S(2)}, u32[]{:S(2)}) %collective-permute-start.6) | collective-permute-done | bytes 2097184 | tf_op jit(solution)/shard_map/ppermute | solution.py:392
  286.5 23.8 %shard_map.51 = (f32[2,2048,256]{2,1,0:T(8,128)}, f32[2,2048,256]{2,1,0:T(8,128)}) custom-call(s32[1]{0:T(128)} %bitcast.flag, f32[2048,256]{1,0:T(8,128)} %get-tuple-element.21.own, f32[2048,256]{1,0:T(8,128)} %collective-permute-done.4.near, f32[2048,256]{1,0:T(8,128)} %collective-permute-done.5.end, f32[2048,256]{1,0:T(8,128)} %collective-permute-done.6.far, ...), custom_call_target="tpu_custom_call" | custom-call | flops 30000001024 | bytes 25165824 | tf_op jit(solution)/shard_map/pallas_call | solution.py:282
  311.6 9.1 %collective-permute-done.11 = f32[2,2048,256]{2,1,0:T(8,128)} collective-permute-done((f32[2,2048,256]{2,1,0:T(8,128)}, f32[2,2048,256]{2,1,0:T(8,128)}, u32[]{:S(2)}, u32[]{:S(2)}) %collective-permute-start.11) | collective-permute-done | bytes 4194336 | tf_op jit(solution)/shard_map/ppermute | solution.py:394
  331.4 43.5 %collective-permute-done.2.far = f32[2048,256]{1,0:T(8,128)} collective-permute-done((f32[2048,256]{1,0:T(8,128)S(1)}, f32[2048,256]{1,0:T(8,128)}, u32[]{:S(2)}, u32[]{:S(2)}) %collective-permute-start.2) | collective-permute-done | bytes 2097184 | tf_op jit(solution)/shard_map/ppermute | solution.py:392
  374.9 23.9 %shard_map.50 = (f32[2,2048,256]{2,1,0:T(8,128)}, f32[2,2048,256]{2,1,0:T(8,128)}) custom-call(s32[1]{0:T(128)} %bitcast.flag, f32[2048,256]{1,0:T(8,128)} %copy-done.2, f32[2048,256]{1,0:T(8,128)} %collective-permute-done.near, f32[2048,256]{1,0:T(8,128)} %collective-permute-done.1.end, f32[2048,256]{1,0:T(8,128)} %collective-permute-done.2.far, ...), custom_call_target="tpu_custom_call" | custom-call | flops 30000001024 | bytes 25165824 | tf_op jit(solution)/shard_map/pallas_call | solution.py:282
  400.2 10.4 %collective-permute-done.7 = f32[2,2048,256]{2,1,0:T(8,128)} collective-permute-done((f32[2,2048,256]{2,1,0:T(8,128)}, f32[2,2048,256]{2,1,0:T(8,128)}, u32[]{:S(2)}, u32[]{:S(2)}) %collective-permute-start.7) | collective-permute-done | bytes 4194336 | tf_op jit(solution)/shard_map/ppermute | solution.py:394
  420.3 76.7 %collective-permute-done.3 = f32[2,2048,256]{2,1,0:T(8,128)} collective-permute-done((f32[2,2048,256]{2,1,0:T(8,128)}, f32[2,2048,256]{2,1,0:T(8,128)}, u32[]{:S(2)}, u32[]{:S(2)}) %collective-permute-start.3) | collective-permute-done | bytes 4194336 | tf_op jit(solution)/shard_map/ppermute | solution.py:394
  510.7 45.2 %all-to-all-done.refs_0_ = f32[8,2,256,256]{3,2,1,0:T(8,128)} async-done(((f32[8,2,256,256]{3,2,1,0:T(8,128)}), f32[8,2,256,256]{3,2,1,0:T(8,128)}, u32[]{:S(2)}, u32[]{:S(2)}) %all-to-all-start) | async-done | bytes 4194336 | tf_op jit(solution)/shard_map/all_to_all | solution.py:397
  555.9 63.7 %shard_map.54 = f32[2,32,256,256]{3,2,1,0:T(8,128)} custom-call(f32[8,2,256,256]{3,2,1,0:T(8,128)} %all-to-all-done.refs_0_, f32[8,2,256,256]{3,2,1,0:T(8,128)} %all-to-all-done.1.refs_1_, f32[8,2,256,256]{3,2,1,0:T(8,128)} %all-to-all-done.2.refs_2_, f32[8,2,256,256]{3,2,1,0:T(8,128)} %all-to-all-done.3.refs_3_, f32[32,256]{1,0:T(8,128)} %get-tuple-element.51.refs_4_, ...), custom_call_target="tpu_custom_call" | custom-call | flops 30000001024 | bytes 33554432 | tf_op jit(solution)/shard_map/pallas_call | solution.py:360
  619.5 17.5 %copy.16 = f32[2,32,256,256]{2,3,1,0:T(8,128)} copy(f32[2,32,256,256]{3,2,1,0:T(8,128)} %shard_map.54) | data formatting | bytes 33554432 | tf_op jit(solution)/shard_map/pallas_call | solution.py:360
  637.0 15.2 %copy.17 = f32[8,2,256,32,32]{2,4,3,1,0:T(8,128)S(1)} copy(f32[8,2,256,32,32]{2,3,0,4,1:T(8,128)} %bitcast.30) | data formatting | bytes 33554432 | tf_op jit(solution)/shard_map/transpose | solution.py:401
  652.2 187.7 %all_to_all.25 = f32[8,2,256,1024]{2,3,1,0:T(8,128)} all-to-all(f32[8,2,256,1024]{2,3,1,0:T(8,128)S(1)} %bitcast.31), channel_id=1, replica_groups=mesh['gx'=8,'gy'=4] {'gx'}, dimensions={0} | all-to-all | bytes 33554432 | tf_op jit(solution)/shard_map/all_to_all | solution.py:403
  840.0 17.7 %copy.18 = f32[2,8,256,1024]{3,2,1,0:T(8,128)} copy(f32[2,8,256,1024]{2,3,0,1:T(8,128)} %bitcast.32) | data formatting | bytes 33554432 | tf_op jit(solution)/shard_map/transpose | solution.py:404
  857.6 9.4 %fusion.61 = (f32[1,64,32,1024]{3,1,2,0:T(8,128)}, f32[1,64,32,1024]{3,1,2,0:T(8,128)S(1)}) fusion(f32[2,64,32,1024]{3,1,2,0:T(8,128)} %bitcast.29), kind=kLoop, calls=%fused_computation.114 | loop fusion | bytes 33554432 | tf_op jit(solution)/shard_map/slice | solution.py:407
  871.9 8.2 copy.20
  880.1 7.7 bitcast_multiply_fusion
  (73 shorter events, 90.3 us)
Async XLA Ops:
  6.9 239.6 %copy-start.2 = (f32[2048,256]{1,0:T(8,128)}, f32[2048,256]{1,0:T(8,128)S(1)}, u32[]{:S(2)}) copy-start(f32[2048,256]{1,0:T(8,128)S(1)} %get-tuple-element.22.own) | copy-start | bytes 6291460
  7.0 20.0 %collective-permute-start.12 = (f32[2048,256]{1,0:T(8,128)}, f32[2048,256]{1,0:T(8,128)}, u32[]{:S(2)}, u32[]{:S(2)}) collective-permute-start(f32[2048,256]{1,0:T(8,128)} %get-tuple-element.20.own), channel_id=1, source_target_pairs={{1,2},{2,1},{5,6},{6,5},{9,10},{10,9},{13,14},{14,13},{17,18},{18,... | collective-permute-start | bytes 6291464 | tf_op jit(solution)/shard_map/ppermute | solution.py:391
  8.9 53.8 %collective-permute-start.13 = (f32[2048,256]{1,0:T(8,128)}, f32[2048,256]{1,0:T(8,128)}, u32[]{:S(2)}, u32[]{:S(2)}) collective-permute-start(f32[2048,256]{1,0:T(8,128)} %get-tuple-element.20.own), channel_id=1, source_target_pairs={{0,1},{3,2},{4,5},{7,6},{8,9},{11,10},{12,13},{15,14},{16,17},{19,... | collective-permute-start | bytes 6291464 | tf_op jit(solution)/shard_map/ppermute | solution.py:390
  16.8 90.0 %collective-permute-start.14 = (f32[2048,256]{1,0:T(8,128)}, f32[2048,256]{1,0:T(8,128)}, u32[]{:S(2)}, u32[]{:S(2)}) collective-permute-start(f32[2048,256]{1,0:T(8,128)} %get-tuple-element.20.own), channel_id=1, source_target_pairs={{0,2},{3,1},{4,6},{7,5},{8,10},{11,9},{12,14},{15,13},{16,18},{19,... | collective-permute-start | bytes 6291464 | tf_op jit(solution)/shard_map/ppermute | solution.py:392
  19.4 132.3 %collective-permute-start.10 = (f32[2048,256]{1,0:T(8,128)}, f32[2048,256]{1,0:T(8,128)}, u32[]{:S(2)}, u32[]{:S(2)}) collective-permute-start(f32[2048,256]{1,0:T(8,128)} %get-tuple-element.23.own), channel_id=1, source_target_pairs={{0,2},{3,1},{4,6},{7,5},{8,10},{11,9},{12,14},{15,13},{16,18},{19,... | collective-permute-start | bytes 6291464 | tf_op jit(solution)/shard_map/ppermute | solution.py:392
  22.0 135.3 %collective-permute-start.8 = (f32[2048,256]{1,0:T(8,128)}, f32[2048,256]{1,0:T(8,128)}, u32[]{:S(2)}, u32[]{:S(2)}) collective-permute-start(f32[2048,256]{1,0:T(8,128)} %get-tuple-element.23.own), channel_id=1, source_target_pairs={{1,2},{2,1},{5,6},{6,5},{9,10},{10,9},{13,14},{14,13},{17,18},{18,... | collective-permute-start | bytes 6291464 | tf_op jit(solution)/shard_map/ppermute | solution.py:391
  27.0 172.8 %collective-permute-start.9 = (f32[2048,256]{1,0:T(8,128)}, f32[2048,256]{1,0:T(8,128)S(1)}, u32[]{:S(2)}, u32[]{:S(2)}) collective-permute-start(f32[2048,256]{1,0:T(8,128)} %get-tuple-element.23.own), channel_id=1, source_target_pairs={{0,1},{3,2},{4,5},{7,6},{8,9},{11,10},{12,13},{15,14},{16,17},{19,... | collective-permute-start | bytes 6291464 | tf_op jit(solution)/shard_map/ppermute | solution.py:390
  134.7 91.9 %collective-permute-start.15 = (f32[2,2048,256]{2,1,0:T(8,128)}, f32[2,2048,256]{2,1,0:T(8,128)}, u32[]{:S(2)}, u32[]{:S(2)}) collective-permute-start(f32[2,2048,256]{2,1,0:T(8,128)} %get-tuple-element.17), channel_id=1, source_target_pairs={{1,0},{2,3},{5,4},{6,7},{9,8},{10,11},{13,12},{14,15},{17,16},{18,... | collective-permute-start | bytes 12582920 | tf_op jit(solution)/shard_map/ppermute | solution.py:394
  136.0 102.3 %collective-permute-start.4 = (f32[2048,256]{1,0:T(8,128)}, f32[2048,256]{1,0:T(8,128)}, u32[]{:S(2)}, u32[]{:S(2)}) collective-permute-start(f32[2048,256]{1,0:T(8,128)} %get-tuple-element.21.own), channel_id=1, source_target_pairs={{1,2},{2,1},{5,6},{6,5},{9,10},{10,9},{13,14},{14,13},{17,18},{18,... | collective-permute-start | bytes 6291464 | tf_op jit(solution)/shard_map/ppermute | solution.py:391
  151.7 94.9 %collective-permute-start.5 = (f32[2048,256]{1,0:T(8,128)}, f32[2048,256]{1,0:T(8,128)}, u32[]{:S(2)}, u32[]{:S(2)}) collective-permute-start(f32[2048,256]{1,0:T(8,128)} %get-tuple-element.21.own), channel_id=1, source_target_pairs={{0,1},{3,2},{4,5},{7,6},{8,9},{11,10},{12,13},{15,14},{16,17},{19,... | collective-permute-start | bytes 6291464 | tf_op jit(solution)/shard_map/ppermute | solution.py:390
  157.3 129.2 %collective-permute-start.6 = (f32[2048,256]{1,0:T(8,128)}, f32[2048,256]{1,0:T(8,128)}, u32[]{:S(2)}, u32[]{:S(2)}) collective-permute-start(f32[2048,256]{1,0:T(8,128)} %get-tuple-element.21.own), channel_id=1, source_target_pairs={{0,2},{3,1},{4,6},{7,5},{8,10},{11,9},{12,14},{15,13},{16,18},{19,... | collective-permute-start | bytes 6291464 | tf_op jit(solution)/shard_map/ppermute | solution.py:392
  225.0 95.7 %collective-permute-start.11 = (f32[2,2048,256]{2,1,0:T(8,128)}, f32[2,2048,256]{2,1,0:T(8,128)}, u32[]{:S(2)}, u32[]{:S(2)}) collective-permute-start(f32[2,2048,256]{2,1,0:T(8,128)} %get-tuple-element.15), channel_id=1, source_target_pairs={{1,0},{2,3},{5,4},{6,7},{9,8},{10,11},{13,12},{14,15},{17,16},{18,... | collective-permute-start | bytes 12582920 | tf_op jit(solution)/shard_map/ppermute | solution.py:394
  226.6 103.8 %collective-permute-start = (f32[2048,256]{1,0:T(8,128)S(1)}, f32[2048,256]{1,0:T(8,128)}, u32[]{:S(2)}, u32[]{:S(2)}) collective-permute-start(f32[2048,256]{1,0:T(8,128)S(1)} %get-tuple-element.22.own), channel_id=1, source_target_pairs={{1,2},{2,1},{5,6},{6,5},{9,10},{10,9},{13,14},{14,13},{17,18},{18,... | collective-permute-start | bytes 6291464 | tf_op jit(solution)/shard_map/ppermute | solution.py:391
  233.8 92.0 %all-to-all-start.3 = ((f32[8,2,256,256]{3,2,1,0:T(8,128)}), f32[8,2,256,256]{3,2,1,0:T(8,128)}, u32[]{:S(2)}, u32[]{:S(2)}) async-start(f32[8,2,256,256]{3,2,1,0:T(8,128)} %bitcast.34), calls=%async_computation.3 | async-start | bytes 8388608 | tf_op jit(solution)/shard_map/all_to_all | solution.py:397
  238.3 82.4 %copy-start = (f32[2,2048,256]{2,1,0:T(8,128)S(1)}, f32[2,2048,256]{2,1,0:T(8,128)}, u32[]{:S(2)}) copy-start(f32[2,2048,256]{2,1,0:T(8,128)} %get-tuple-element.14) | copy-start | bytes 12582916
  238.4 93.0 %collective-permute-start.1 = (f32[2048,256]{1,0:T(8,128)S(1)}, f32[2048,256]{1,0:T(8,128)}, u32[]{:S(2)}, u32[]{:S(2)}) collective-permute-start(f32[2048,256]{1,0:T(8,128)S(1)} %get-tuple-element.22.own), channel_id=1, source_target_pairs={{0,1},{3,2},{4,5},{7,6},{8,9},{11,10},{12,13},{15,14},{16,17},{19,... | collective-permute-start | bytes 6291464 | tf_op jit(solution)/shard_map/ppermute | solution.py:390
  246.6 128.3 %collective-permute-start.2 = (f32[2048,256]{1,0:T(8,128)S(1)}, f32[2048,256]{1,0:T(8,128)}, u32[]{:S(2)}, u32[]{:S(2)}) collective-permute-start(f32[2048,256]{1,0:T(8,128)S(1)} %get-tuple-element.22.own), channel_id=1, source_target_pairs={{0,2},{3,1},{4,6},{7,5},{8,10},{11,9},{12,14},{15,13},{16,18},{19,... | collective-permute-start | bytes 6291464 | tf_op jit(solution)/shard_map/ppermute | solution.py:392
  310.3 100.3 %collective-permute-start.7 = (f32[2,2048,256]{2,1,0:T(8,128)}, f32[2,2048,256]{2,1,0:T(8,128)}, u32[]{:S(2)}, u32[]{:S(2)}) collective-permute-start(f32[2,2048,256]{2,1,0:T(8,128)} %get-tuple-element.13), channel_id=1, source_target_pairs={{1,0},{2,3},{5,4},{6,7},{9,8},{10,11},{13,12},{14,15},{17,16},{18,... | collective-permute-start | bytes 12582920 | tf_op jit(solution)/shard_map/ppermute | solution.py:394
  325.8 89.9 %all-to-all-start.2 = ((f32[8,2,256,256]{3,2,1,0:T(8,128)}), f32[8,2,256,256]{3,2,1,0:T(8,128)}, u32[]{:S(2)}, u32[]{:S(2)}) async-start(f32[8,2,256,256]{3,2,1,0:T(8,128)} %bitcast.33), calls=%async_computation.2 | async-start | bytes 8388608 | tf_op jit(solution)/shard_map/all_to_all | solution.py:397
  330.4 80.2 %copy-start.1 = (f32[2,2048,256]{2,1,0:T(8,128)S(1)}, f32[2,2048,256]{2,1,0:T(8,128)}, u32[]{:S(2)}) copy-start(f32[2,2048,256]{2,1,0:T(8,128)} %get-tuple-element.12) | copy-start | bytes 12582916
  398.8 98.2 %collective-permute-start.3 = (f32[2,2048,256]{2,1,0:T(8,128)}, f32[2,2048,256]{2,1,0:T(8,128)}, u32[]{:S(2)}, u32[]{:S(2)}) collective-permute-start(f32[2,2048,256]{2,1,0:T(8,128)} %get-tuple-element.11), channel_id=1, source_target_pairs={{1,0},{2,3},{5,4},{6,7},{9,8},{10,11},{13,12},{14,15},{17,16},{18,... | collective-permute-start | bytes 12582920 | tf_op jit(solution)/shard_map/ppermute | solution.py:394
  415.7 86.4 %all-to-all-start.1 = ((f32[8,2,256,256]{3,2,1,0:T(8,128)}), f32[8,2,256,256]{3,2,1,0:T(8,128)}, u32[]{:S(2)}, u32[]{:S(2)}) async-start(f32[8,2,256,256]{3,2,1,0:T(8,128)} %bitcast.36), calls=%async_computation.1 | async-start | bytes 8388608 | tf_op jit(solution)/shard_map/all_to_all | solution.py:397
  502.2 53.7 %all-to-all-start = ((f32[8,2,256,256]{3,2,1,0:T(8,128)}), f32[8,2,256,256]{3,2,1,0:T(8,128)}, u32[]{:S(2)}, u32[]{:S(2)}) async-start(f32[8,2,256,256]{3,2,1,0:T(8,128)} %bitcast.35), calls=%async_computation | async-start | bytes 8388608 | tf_op jit(solution)/shard_map/all_to_all | solution.py:397
  871.8 8.3 copy-start.3
  (2 other events, 9.6 us)

commit v2 on v1

--- a/solution.py
+++ b/solution.py
@@ -317,19 +317,25 @@
 
 
 def columns_kernel(*refs):
-    parts = refs[:4]
-    cosine, sine, table_high, table_low, out, high, low = refs[4:]
-    groups, _, rows, depth = parts[0].shape
+    parts = refs[:-7]
+    cosine, sine, table_high, table_low, out, high, low = refs[-7:]
+    rows = parts[0].shape[2]
+    depth = cosine.shape[1]
+    pieces = [(m, lane) for m in range(len(parts)) for lane in range(0, parts[m].shape[3], 128)]
+    per_group = depth // 128
 
     @pl.loop(0, rows // 16)
     def _(step):
-        here = pl.ds(pl.multiple_of(step * 16, 16), 16)
+        start = pl.multiple_of(step * 16, 16)
+        here = pl.ds(start, 16)
         for lane in range(0, depth, 128):
             lanes = pl.ds(lane, 128)
-            values = [
-                (parts[q % 4][q // 4, 0, here, lanes], parts[q % 4][q // 4, 1, here, lanes])
-                for q in range(RADIX)
-            ]
+            values = []
+            for q in range(RADIX):
+                m, offset = pieces[q % 4 * per_group + lane // 128]
+                values.append(
+                    tuple(parts[m][q // 4, t, here, pl.ds(offset, 128)] for t in range(2))
+                )
             spectrum = small_dft(values, RADIX)
             for k in range(RADIX):
                 real, imag = spectrum[k]
@@ -337,18 +343,22 @@
                     c = cosine[pl.ds(k, 1), lanes]
                     s = sine[pl.ds(k, 1), lanes]
                     real, imag = real * c - imag * s, real * s + imag * c
-                split_store(high, low, (k, here, lanes), real)
-                split_store(high, low, (k, here, pl.ds(depth + lane, 128)), imag)
-
-    @pl.loop(0, RADIX)
+                there = pl.ds(pl.multiple_of(k * rows + start, 16), 16)
+                split_store(high, low, (there, lanes), real)
+                split_store(high, low, (there, pl.ds(depth + lane, 128)), imag)
+
+    some = 8
+
+    @pl.loop(0, RADIX // some)
     def _(k):
-        result = product(high[k], low[k], table_high[...], table_low[...])
-        out[0, k] = result[:, :depth]
-        out[1, k] = result[:, depth:]
-
-
-def columns_stage(parts, length):
-    groups, _, rows, depth = parts[0].shape
+        here = pl.ds(pl.multiple_of(k * some * rows, 16), some * rows)
+        result = product(high[here, :], low[here, :], table_high[...], table_low[...])
+        out[0, here, :] = result[:, :depth]
+        out[1, here, :] = result[:, depth:]
+
+
+def columns_tables(length):
+    depth = length // RADIX
     p = jnp.arange(depth, dtype=jnp.int32)
     k = jnp.arange(RADIX, dtype=jnp.int32)
     cosine, sine = unit_angle(k[:, None] * p[None, :], length)
@@ -356,22 +366,62 @@
     table = jnp.concatenate(
         [jnp.concatenate([c, s], axis=1), jnp.concatenate([-s, c], axis=1)], axis=0
     )
-    tile = 64
+    return (cosine, sine) + halves(table)
+
+
+def columns_stage(parts, tables, piece, tile):
+    groups = parts[0].shape[0]
+    depth = tables[0].shape[1]
     return pl.pallas_call(
         columns_kernel,
-        grid=(rows // tile,),
-        out_shape=jax.ShapeDtypeStruct((2, RADIX, rows, depth), jnp.float32),
-        in_specs=[pl.BlockSpec((groups, 2, tile, depth), lambda i: (0, 0, i, 0))] * 4 + [FULL] * 4,
-        out_specs=pl.BlockSpec((2, RADIX, tile, depth), lambda i: (0, 0, i, 0)),
+        grid=(1,),
+        out_shape=jax.ShapeDtypeStruct((2, RADIX * tile, depth), jnp.float32),
+        in_specs=[
+            pl.BlockSpec((groups, 2, tile, part.shape[3]), lambda i: (0, 0, piece, 0))
+            for part in parts
+        ]
+        + [FULL] * 4,
+        out_specs=pl.BlockSpec((2, RADIX * tile, depth), lambda i: (0, 0, 0)),
         scratch_shapes=[
-            VMEM((RADIX, tile, 2 * depth), jnp.bfloat16),
-            VMEM((RADIX, tile, 2 * depth), jnp.bfloat16),
+            VMEM((RADIX * tile, 2 * depth), jnp.bfloat16),
+            VMEM((RADIX * tile, 2 * depth), jnp.bfloat16),
         ],
         compiler_params=pltpu.CompilerParams(vmem_limit_bytes=56 * 2**20),
         cost_estimate=pl.CostEstimate(
-            flops=30 * 10**9, bytes_accessed=32 * 2**20, transcendentals=0
+            flops=8 * 10**9, bytes_accessed=8 * 2**20, transcendentals=0
         ),
-    )(*parts, cosine, sine, *halves(table))
+    )(*parts, *tables)
+
+
+def finish_kernel(*refs):
+    pieces = refs[:-4]
+    by_row, by_column, real_out, imag_out = refs[-4:]
+    groups, _, some, width = pieces[0].shape
+    count = groups * len(pieces)
+    for t, out in enumerate((real_out, imag_out)):
+        for lane in range(0, width, 128):
+            lanes = pl.ds(lane, 128)
+            rows = [pieces[k % len(pieces)][k // len(pieces), t, :, lanes] for k in range(count)]
+            turned = jnp.transpose(jnp.stack(rows, axis=0), (1, 0, 2))
+            turned = turned.reshape(some * count, 128)
+            out[:, lanes] = turned * (by_row[...] * by_column[:, lanes])
+
+
+def finish_stage(pieces, by_row, by_column):
+    groups, _, rows, width = pieces[0].shape
+    some = 8
+    tall = some * groups * len(pieces)
+    shape = jax.ShapeDtypeStruct((rows * groups * len(pieces), width), jnp.float32)
+    out_spec = pl.BlockSpec((tall, width), lambda i: (i, 0))
+    return pl.pallas_call(
+        finish_kernel,
+        grid=(rows // some,),
+        out_shape=(shape, shape),
+        in_specs=[pl.BlockSpec((groups, 2, some, width), lambda i: (0, 0, i, 0))] * len(pieces)
+        + [pl.BlockSpec((tall, 128), lambda i: (i, 0)), pl.BlockSpec((1, width), lambda i: (0, 0))],
+        out_specs=(out_spec, out_spec),
+        compiler_params=pltpu.CompilerParams(vmem_limit_bytes=48 * 2**20),
+    )(*pieces, by_row, by_column)
 
 
 def line_transform(density, kernel_rows, kernel_cols, blocks, groups):
@@ -385,26 +435,31 @@
     tables = rows_tables(place, length, blocks)
     chunk = columns // RADIX
     parts = []
-    for m in range(width // chunk):
-        own = density[:, m * chunk : (m + 1) * chunk]
+    begin = 0
+    for size in [chunk] * (width // chunk - 1) + [chunk // 2] * 2:
+        own = density[:, begin : begin + size]
+        begin += size
         end = lax.ppermute(own, "gy", [(0, 1), (3, 2)])
         near = lax.ppermute(own, "gy", [(1, 2), (2, 1)])
         far = lax.ppermute(own, "gy", [(0, 2), (3, 1)])
         kept, sent = rows_stage(flag, own, near, end, far, tables)
         given = lax.ppermute(sent, "gy", [(1, 0), (2, 3)])
         mine = jnp.where(inner, kept, given)
-        mine = mine.reshape(2, groups, rows_here // groups, chunk).transpose(1, 0, 2, 3)
+        mine = mine.reshape(2, groups, rows_here // groups, size).transpose(1, 0, 2, 3)
         parts.append(lax.all_to_all(mine, "gx", split_axis=0, concat_axis=0, tiled=True))
-    result = columns_stage(parts, columns)
     rows_part = rows_here // groups
     share = chunk // groups
-    result = result.reshape(2, RADIX, rows_part, groups, share).transpose(3, 0, 2, 4, 1)
-    result = result.reshape(groups, 2, rows_part, width)
-    result = lax.all_to_all(result, "gx", split_axis=0, concat_axis=0, tiled=True)
-    result = result.transpose(1, 0, 2, 3).reshape(2, RADIX, rows_here // RADIX, width)
-    result = result.transpose(0, 2, 1, 3).reshape(2, rows_here, width)
-    factor = kernel_rows[:, None] * kernel_cols[None, :] * (1.0 / math.sqrt(length * columns))
-    return (result[0] * factor, result[1] * factor)
+    tile = rows_here // RADIX
+    tables = columns_tables(columns)
+    pieces = []
+    for piece in range(rows_part // tile):
+        result = columns_stage(parts, tables, piece, tile)
+        result = result.reshape(2, RADIX, tile, groups, share).transpose(3, 0, 2, 4, 1)
+        result = result.reshape(groups, 2, tile, width)
+        pieces.append(lax.all_to_all(result, "gx", split_axis=0, concat_axis=0, tiled=True))
+    scale = kernel_rows * (1.0 / math.sqrt(length * columns))
+    by_row = jnp.broadcast_to(scale[:, None], (rows_here, 128))
+    return finish_stage(pieces, by_row, kernel_cols[None, :])
 
 
 def solution(mesh):

time: 889 us -> 902 us (1.015)
  blocking collectives: 188 us -> 0 us
  waiting for transfers between devices: 281 us -> 454 us
  starting transfers between devices: 139 us -> 158 us
    all_to_all x1 -> x0, blocking collectives: 188 us -> none  [line_transform(): lax.all_to_all(result, 'gx', split_axis=0, concat_axis=0, tiled=True)]
    ppermute x4 -> x5, waiting for transfers between devices: 96.4 us -> 203 us  [line_transform(): given = lax.ppermute(sent, 'gy', [(1, 0), (2, 3)])]
    all_to_all x0 -> x4, waiting for transfers between devices: none -> 104 us  [line_transform(): lax.all_to_all(result, 'gx', split_axis=0, concat_axis=0, tiled=True)]
    ppermute x4 -> x5, waiting for transfers between devices: 138 us -> 51.1 us  [line_transform(): far = lax.ppermute(own, 'gy', [(0, 2), (3, 1)])]
    reshape x4 -> x13, local copies, waits for them, and re-layouts: 9.63 us -> 68.5 us  [the longest x4 31.2 us: line_transform(): result.reshape(2, RADIX, tile, groups, share).transpose(3, 0, 2, 4, 1)]
    ppermute x4 -> x5, waiting for transfers between devices: 0.99 us -> 50.8 us  [line_transform(): end = lax.ppermute(own, 'gy', [(0, 1), (3, 2)])]
    ppermute x4 -> x5, starting transfers between devices: 50.3 us -> 16.2 us  [line_transform(): far = lax.ppermute(own, 'gy', [(0, 2), (3, 1)])]
    transpose x2 -> x0, local copies, waits for them, and re-layouts: 32.9 us -> none  [the longest x1 17.7 us: line_transform(): result.transpose(1, 0, 2, 3).reshape(2, RADIX, rows_here // RADIX, width)]
  transfers between devices with their start and end apart: 20 -> 29, of which waited for: 10 -> 14; matrix products, arithmetic and copies ran while one was open for 4% -> 10% of each run, Pallas kernels for 11% -> 16%
where the time goes in v2:
time: 902 us; the launch traced here: 899 us
  waiting for transfers between devices  454 us (50%)
  Pallas kernels  166 us (18%)
  starting transfers between devices  158 us (18%)
  local copies, waits for them, and re-layouts  103 us (11%)
  other arithmetic  18.4 us (2%)
    ppermute x5, waiting for transfers between devices, line_transform(): given = lax.ppermute(sent, 'gy', [(1, 0), (2, 3)])  203 us
    pallas_call x5, Pallas kernels, rows_stage(): pl.pallas_call(rows_kernel, out_shape=(shape, shape), in_specs=[pl.BlockS...  108 us
    all_to_all x4, waiting for transfers between devices, line_transform(): lax.all_to_all(result, 'gx', split_axis=0, concat_axis=0, tiled=True)  104 us
    ppermute x5, starting transfers between devices, line_transform(): end = lax.ppermute(own, 'gy', [(0, 1), (3, 2)])  86.4 us
    ppermute x5, waiting for transfers between devices, line_transform(): far = lax.ppermute(own, 'gy', [(0, 2), (3, 1)])  51.1 us
    ppermute x5, waiting for transfers between devices, line_transform(): end = lax.ppermute(own, 'gy', [(0, 1), (3, 2)])  50.8 us
    all_to_all x5, waiting for transfers between devices, line_transform(): lax.all_to_all(mine, 'gx', split_axis=0, concat_axis=0, tiled=True)  45.2 us
    pallas_call x4, Pallas kernels, columns_stage(): pl.pallas_call(columns_kernel, grid=(1,), out_shape=jax.ShapeDtypeStruct(...  43.9 us
  transfers between devices with their start and end apart: 29, of which 14 were waited for; matrix products, arithmetic and copies ran while one was open for 10% of the time, Pallas kernels for 16%

profile of v2, /device:TPU:0, one launch (start us, length us, event | category | flops | bytes accessed | tf_op | source)
XLA Modules:
  0.0 899.2 jit_solution(5521803173424238455)
XLA Ops:
  30.2 50.8 %collective-permute-done.13.end = f32[2048,128]{1,0:T(8,128)} collective-permute-done((f32[2048,128]{1,0:T(8,128)S(1)}, f32[2048,128]{1,0:T(8,128)}, u32[]{:S(2)}, u32[]{:S(2)}) %collective-permute-start.13) | collective-permute-done | bytes 1048608 | tf_op jit(solution)/shard_map/ppermute | solution.py:442
  81.0 74.2 %collective-permute-start.17 = (f32[2048,128]{1,0:T(8,128)S(1)}, f32[2048,128]{1,0:T(8,128)S(1)}, u32[]{:S(2)}, u32[]{:S(2)}) collective-permute-start(f32[2048,128]{1,0:T(8,128)S(1)} %get-tuple-element.22.own), channel_id=1, source_target_pairs={{0,1},{3,2},{4,5},{7,6},{8,9},{11,10},{12,13},{15,14},{16,17},{19,... | collective-permute-start | bytes 3145736 | tf_op jit(solution)/shard_map/ppermute | solution.py:442
  160.6 18.0 %shard_map.53 = (f32[2,2048,128]{2,1,0:T(8,128)}, f32[2,2048,128]{2,1,0:T(8,128)}) custom-call(s32[1]{0:T(128)} %bitcast.flag, f32[2048,128]{1,0:T(8,128)} %copy-done.7, f32[2048,128]{1,0:T(8,128)} %collective-permute-done.12.near, f32[2048,128]{1,0:T(8,128)} %collective-permute-done.13.end, f32[2048,128]{1,0:T(8,128)} %collective-permute-done.14.far, ...), custom_call_target="tpu_custom_call" | custom-call | flops 30000001024 | bytes 25165824 | tf_op jit(solution)/shard_map/pallas_call | solution.py:282
  183.3 17.9 %collective-permute-done.18.far = f32[2048,128]{1,0:T(8,128)S(1)} collective-permute-done((f32[2048,128]{1,0:T(8,128)S(1)}, f32[2048,128]{1,0:T(8,128)S(1)}, u32[]{:S(2)}, u32[]{:S(2)}) %collective-permute-start.18) | collective-permute-done | bytes 1048608 | tf_op jit(solution)/shard_map/ppermute | solution.py:444
  203.6 18.0 %shard_map.54 = (f32[2,2048,128]{2,1,0:T(8,128)}, f32[2,2048,128]{2,1,0:T(8,128)}) custom-call(s32[1]{0:T(128)} %bitcast.flag, f32[2048,128]{1,0:T(8,128)} %copy-done.6, f32[2048,128]{1,0:T(8,128)} %copy-done.10, f32[2048,128]{1,0:T(8,128)} %copy-done.11, f32[2048,128]{1,0:T(8,128)} %copy-done.12, f32[17,256,128]{2,1,0:T(8,128)} %broadcast_in_dim.24.cosine, ...), custom_call_target="tpu_custom_call" | custom-call | flops 30000001024 | bytes 25165824 | tf_op jit(solution)/shard_map/pallas_call | solution.py:282
  221.6 27.9 %collective-permute-done.15 = f32[2,2048,128]{2,1,0:T(8,128)S(1)} collective-permute-done((f32[2,2048,128]{2,1,0:T(8,128)}, f32[2,2048,128]{2,1,0:T(8,128)S(1)}, u32[]{:S(2)}, u32[]{:S(2)}) %collective-permute-start.15) | collective-permute-done | bytes 2097184 | tf_op jit(solution)/shard_map/ppermute | solution.py:446
  261.9 23.9 %shard_map.52 = (f32[2,2048,256]{2,1,0:T(8,128)}, f32[2,2048,256]{2,1,0:T(8,128)}) custom-call(s32[1]{0:T(128)} %bitcast.flag, f32[2048,256]{1,0:T(8,128)} %get-tuple-element.24.own, f32[2048,256]{1,0:T(8,128)} %collective-permute-done.8.near, f32[2048,256]{1,0:T(8,128)} %collective-permute-done.9.end, f32[2048,256]{1,0:T(8,128)} %collective-permute-done.10.far, ...), custom_call_target="tpu_custom_call" | custom-call | flops 30000001024 | bytes 25165824 | tf_op jit(solution)/shard_map/pallas_call | solution.py:282
  287.1 24.0 %collective-permute-done.19 = f32[2,2048,128]{2,1,0:T(8,128)S(1)} collective-permute-done((f32[2,2048,128]{2,1,0:T(8,128)}, f32[2,2048,128]{2,1,0:T(8,128)S(1)}, u32[]{:S(2)}, u32[]{:S(2)}) %collective-permute-start.19) | collective-permute-done | bytes 2097184 | tf_op jit(solution)/shard_map/ppermute | solution.py:446
  326.2 16.2 %collective-permute-done.6.far = f32[2048,256]{1,0:T(8,128)} collective-permute-done((f32[2048,256]{1,0:T(8,128)}, f32[2048,256]{1,0:T(8,128)}, u32[]{:S(2)}, u32[]{:S(2)}) %collective-permute-start.6) | collective-permute-done | bytes 2097184 | tf_op jit(solution)/shard_map/ppermute | solution.py:444
  342.4 23.9 %shard_map.51 = (f32[2,2048,256]{2,1,0:T(8,128)}, f32[2,2048,256]{2,1,0:T(8,128)}) custom-call(s32[1]{0:T(128)} %bitcast.flag, f32[2048,256]{1,0:T(8,128)} %get-tuple-element.25.own, f32[2048,256]{1,0:T(8,128)} %collective-permute-done.4.near, f32[2048,256]{1,0:T(8,128)} %collective-permute-done.5.end, f32[2048,256]{1,0:T(8,128)} %collective-permute-done.6.far, ...), custom_call_target="tpu_custom_call" | custom-call | flops 30000001024 | bytes 25165824 | tf_op jit(solution)/shard_map/pallas_call | solution.py:282
  367.6 33.4 %collective-permute-done.11 = f32[2,2048,256]{2,1,0:T(8,128)} collective-permute-done((f32[2,2048,256]{2,1,0:T(8,128)}, f32[2,2048,256]{2,1,0:T(8,128)}, u32[]{:S(2)}, u32[]{:S(2)}) %collective-permute-start.11) | collective-permute-done | bytes 4194336 | tf_op jit(solution)/shard_map/ppermute | solution.py:446
  411.0 17.0 %collective-permute-done.2.far = f32[2048,256]{1,0:T(8,128)} collective-permute-done((f32[2048,256]{1,0:T(8,128)}, f32[2048,256]{1,0:T(8,128)}, u32[]{:S(2)}, u32[]{:S(2)}) %collective-permute-start.2) | collective-permute-done | bytes 2097184 | tf_op jit(solution)/shard_map/ppermute | solution.py:444
  428.0 23.9 %shard_map.50 = (f32[2,2048,256]{2,1,0:T(8,128)}, f32[2,2048,256]{2,1,0:T(8,128)}) custom-call(s32[1]{0:T(128)} %bitcast.flag, f32[2048,256]{1,0:T(8,128)} %get-tuple-element.26.own, f32[2048,256]{1,0:T(8,128)} %collective-permute-done.near, f32[2048,256]{1,0:T(8,128)} %collective-permute-done.1.end, f32[2048,256]{1,0:T(8,128)} %collective-permute-done.2.far, ...), custom_call_target="tpu_custom_call" | custom-call | flops 30000001024 | bytes 25165824 | tf_op jit(solution)/shard_map/pallas_call | solution.py:282
  453.2 37.8 %collective-permute-done.7 = f32[2,2048,256]{2,1,0:T(8,128)} collective-permute-done((f32[2,2048,256]{2,1,0:T(8,128)}, f32[2,2048,256]{2,1,0:T(8,128)}, u32[]{:S(2)}, u32[]{:S(2)}) %collective-permute-start.7) | collective-permute-done | bytes 4194336 | tf_op jit(solution)/shard_map/ppermute | solution.py:446
  500.7 79.7 %collective-permute-done.3 = f32[2,2048,256]{2,1,0:T(8,128)} collective-permute-done((f32[2,2048,256]{2,1,0:T(8,128)}, f32[2,2048,256]{2,1,0:T(8,128)}, u32[]{:S(2)}, u32[]{:S(2)}) %collective-permute-start.3) | collective-permute-done | bytes 4194336 | tf_op jit(solution)/shard_map/ppermute | solution.py:446
  594.1 45.2 %all-to-all-done.refs_0_ = f32[8,2,256,256]{3,2,1,0:T(8,128)} async-done(((f32[8,2,256,256]{3,2,1,0:T(8,128)}), f32[8,2,256,256]{3,2,1,0:T(8,128)}, u32[]{:S(2)}, u32[]{:S(2)}) %all-to-all-start) | async-done | bytes 4194336 | tf_op jit(solution)/shard_map/all_to_all | solution.py:449
  675.0 11.0 %shard_map.57 = f32[2,2048,256]{2,1,0:T(8,128)} custom-call(f32[8,2,256,256]{3,2,1,0:T(8,128)} %all-to-all-done.refs_0_, f32[8,2,256,256]{3,2,1,0:T(8,128)} %all-to-all-done.1.refs_1_, f32[8,2,256,256]{3,2,1,0:T(8,128)} %all-to-all-done.2.refs_2_, f32[8,2,256,128]{3,2,1,0:T(8,128)} %copy-done.5, f32[8,2,256,128]{3,2,1,0:T(8,128)} %all-to-all-done.4.refs_4_, ...), custom_call_target="tpu_custom_call" | custom-call | flops 8000000000 | bytes 8388608 | tf_op jit(solution)/shard_map/pallas_call | solution.py:375
  706.0 18.0 %all-to-all-done.8.refs_3_ = f32[8,2,64,1024]{3,2,1,0:T(8,128)} async-done(((f32[8,2,64,1024]{3,2,1,0:T(8,128)}), f32[8,2,64,1024]{3,2,1,0:T(8,128)}, u32[]{:S(2)}, u32[]{:S(2)}) %all-to-all-start.8) | async-done | bytes 4194336 | tf_op jit(solution)/shard_map/all_to_all | solution.py:459
  728.5 11.0 %shard_map.56 = f32[2,2048,256]{2,1,0:T(8,128)} custom-call(f32[8,2,256,256]{3,2,1,0:T(8,128)} %all-to-all-done.refs_0_, f32[8,2,256,256]{3,2,1,0:T(8,128)} %all-to-all-done.1.refs_1_, f32[8,2,256,256]{3,2,1,0:T(8,128)} %all-to-all-done.2.refs_2_, f32[8,2,256,128]{3,2,1,0:T(8,128)} %copy-done.5, f32[8,2,256,128]{3,2,1,0:T(8,128)} %all-to-all-done.4.refs_4_, ...), custom_call_target="tpu_custom_call" | custom-call | flops 8000000000 | bytes 8388608 | tf_op jit(solution)/shard_map/pallas_call | solution.py:375
  759.4 18.2 %all-to-all-done.7.refs_2_ = f32[8,2,64,1024]{3,2,1,0:T(8,128)} async-done(((f32[8,2,64,1024]{3,2,1,0:T(8,128)}), f32[8,2,64,1024]{3,2,1,0:T(8,128)}, u32[]{:S(2)}, u32[]{:S(2)}) %all-to-all-start.7) | async-done | bytes 4194336 | tf_op jit(solution)/shard_map/all_to_all | solution.py:459
  782.2 11.0 %shard_map.55 = f32[2,2048,256]{2,1,0:T(8,128)} custom-call(f32[8,2,256,256]{3,2,1,0:T(8,128)} %all-to-all-done.refs_0_, f32[8,2,256,256]{3,2,1,0:T(8,128)} %all-to-all-done.1.refs_1_, f32[8,2,256,256]{3,2,1,0:T(8,128)} %all-to-all-done.2.refs_2_, f32[8,2,256,128]{3,2,1,0:T(8,128)} %copy-done.5, f32[8,2,256,128]{3,2,1,0:T(8,128)} %all-to-all-done.4.refs_4_, ...), custom_call_target="tpu_custom_call" | custom-call | flops 8000000000 | bytes 8388608 | tf_op jit(solution)/shard_map/pallas_call | solution.py:375
  813.1 18.2 %all-to-all-done.6.refs_1_ = f32[8,2,64,1024]{3,2,1,0:T(8,128)} async-done(((f32[8,2,64,1024]{3,2,1,0:T(8,128)}), f32[8,2,64,1024]{3,2,1,0:T(8,128)}, u32[]{:S(2)}, u32[]{:S(2)}) %all-to-all-start.6) | async-done | bytes 4194336 | tf_op jit(solution)/shard_map/all_to_all | solution.py:459
  835.9 49.1 %all-to-all-done.5.refs_0_ = f32[8,2,64,1024]{3,2,1,0:T(8,128)} async-done(((f32[8,2,64,1024]{3,2,1,0:T(8,128)}), f32[8,2,64,1024]{3,2,1,0:T(8,128)}, u32[]{:S(2)}, u32[]{:S(2)}) %all-to-all-start.5) | async-done | bytes 4194336 | tf_op jit(solution)/shard_map/all_to_all | solution.py:459
  885.3 13.9 %shard_map.59 = (f32[2048,1024]{1,0:T(8,128)}, f32[2048,1024]{1,0:T(8,128)}) custom-call(f32[8,2,64,1024]{3,2,1,0:T(8,128)} %all-to-all-done.5.refs_0_, f32[8,2,64,1024]{3,2,1,0:T(8,128)} %all-to-all-done.6.refs_1_, f32[8,2,64,1024]{3,2,1,0:T(8,128)} %all-to-all-done.7.refs_2_, f32[8,2,64,1024]{3,2,1,0:T(8,128)} %all-to-all-done.8.refs_3_, ...), custom_call_target="tpu_custom_call" | custom-call | tf_op jit(solution)/shard_map/pallas_call | solution.py:416
  (119 shorter events, 215.9 us)
Async XLA Ops:
  6.3 251.5 %collective-permute-start.10 = (f32[2048,256]{1,0:T(8,128)}, f32[2048,256]{1,0:T(8,128)}, u32[]{:S(2)}, u32[]{:S(2)}) collective-permute-start(f32[2048,256]{1,0:T(8,128)} %get-tuple-element.24.own), channel_id=1, source_target_pairs={{0,2},{3,1},{4,6},{7,5},{8,10},{11,9},{12,14},{15,13},{16,18},{19,... | collective-permute-start | bytes 6291464 | tf_op jit(solution)/shard_map/ppermute | solution.py:444
  13.5 246.9 %collective-permute-start.8 = (f32[2048,256]{1,0:T(8,128)}, f32[2048,256]{1,0:T(8,128)}, u32[]{:S(2)}, u32[]{:S(2)}) collective-permute-start(f32[2048,256]{1,0:T(8,128)} %get-tuple-element.24.own), channel_id=1, source_target_pairs={{1,2},{2,1},{5,6},{6,5},{9,10},{10,9},{13,14},{14,13},{17,18},{18,... | collective-permute-start | bytes 6291464 | tf_op jit(solution)/shard_map/ppermute | solution.py:443
  18.9 62.1 %collective-permute-start.13 = (f32[2048,128]{1,0:T(8,128)S(1)}, f32[2048,128]{1,0:T(8,128)}, u32[]{:S(2)}, u32[]{:S(2)}) collective-permute-start(f32[2048,128]{1,0:T(8,128)S(1)} %get-tuple-element.23.own), channel_id=1, source_target_pairs={{0,1},{3,2},{4,5},{7,6},{8,9},{11,10},{12,13},{15,14},{16,17},{19,... | collective-permute-start | bytes 3145736 | tf_op jit(solution)/shard_map/ppermute | solution.py:442
  21.2 133.9 %collective-permute-start.14 = (f32[2048,128]{1,0:T(8,128)S(1)}, f32[2048,128]{1,0:T(8,128)}, u32[]{:S(2)}, u32[]{:S(2)}) collective-permute-start(f32[2048,128]{1,0:T(8,128)S(1)} %get-tuple-element.23.own), channel_id=1, source_target_pairs={{0,2},{3,1},{4,6},{7,5},{8,10},{11,9},{12,14},{15,13},{16,18},{19,... | collective-permute-start | bytes 3145736 | tf_op jit(solution)/shard_map/ppermute | solution.py:444
  29.4 149.2 %collective-permute-start.16 = (f32[2048,128]{1,0:T(8,128)S(1)}, f32[2048,128]{1,0:T(8,128)S(1)}, u32[]{:S(2)}, u32[]{:S(2)}) collective-permute-start(f32[2048,128]{1,0:T(8,128)S(1)} %get-tuple-element.22.own), channel_id=1, source_target_pairs={{1,2},{2,1},{5,6},{6,5},{9,10},{10,9},{13,14},{14,13},{17,18},{18,... | collective-permute-start | bytes 3145736 | tf_op jit(solution)/shard_map/ppermute | solution.py:443
  81.0 100.3 %collective-permute-start.17 = (f32[2048,128]{1,0:T(8,128)S(1)}, f32[2048,128]{1,0:T(8,128)S(1)}, u32[]{:S(2)}, u32[]{:S(2)}) collective-permute-start(f32[2048,128]{1,0:T(8,128)S(1)} %get-tuple-element.22.own), channel_id=1, source_target_pairs={{0,1},{3,2},{4,5},{7,6},{8,9},{11,10},{12,13},{15,14},{16,17},{19,... | collective-permute-start | bytes 3145736 | tf_op jit(solution)/shard_map/ppermute | solution.py:442
  178.6 83.3 %collective-permute-start.9 = (f32[2048,256]{1,0:T(8,128)}, f32[2048,256]{1,0:T(8,128)}, u32[]{:S(2)}, u32[]{:S(2)}) collective-permute-start(f32[2048,256]{1,0:T(8,128)} %get-tuple-element.24.own), channel_id=1, source_target_pairs={{0,1},{3,2},{4,5},{7,6},{8,9},{11,10},{12,13},{15,14},{16,17},{19,... | collective-permute-start | bytes 6291464 | tf_op jit(solution)/shard_map/ppermute | solution.py:442
  181.3 133.5 %collective-permute-start.4 = (f32[2048,256]{1,0:T(8,128)}, f32[2048,256]{1,0:T(8,128)}, u32[]{:S(2)}, u32[]{:S(2)}) collective-permute-start(f32[2048,256]{1,0:T(8,128)} %get-tuple-element.25.own), channel_id=1, source_target_pairs={{1,2},{2,1},{5,6},{6,5},{9,10},{10,9},{13,14},{14,13},{17,18},{18,... | collective-permute-start | bytes 6291464 | tf_op jit(solution)/shard_map/ppermute | solution.py:443
  249.5 69.7 %collective-permute-start.5 = (f32[2048,256]{1,0:T(8,128)}, f32[2048,256]{1,0:T(8,128)}, u32[]{:S(2)}, u32[]{:S(2)}) collective-permute-start(f32[2048,256]{1,0:T(8,128)} %get-tuple-element.25.own), channel_id=1, source_target_pairs={{0,1},{3,2},{4,5},{7,6},{8,9},{11,10},{12,13},{15,14},{16,17},{19,... | collective-permute-start | bytes 6291464 | tf_op jit(solution)/shard_map/ppermute | solution.py:442
  254.0 67.8 %all-to-all-start.3 = ((f32[8,2,256,128]{3,2,1,0:T(8,128)}), f32[8,2,256,128]{3,2,1,0:T(8,128)S(1)}, u32[]{:S(2)}, u32[]{:S(2)}) async-start(f32[8,2,256,128]{3,2,1,0:T(8,128)} %bitcast.41), calls=%async_computation.3 | async-start | bytes 4194304 | tf_op jit(solution)/shard_map/all_to_all | solution.py:449
  257.8 84.7 %collective-permute-start.6 = (f32[2048,256]{1,0:T(8,128)}, f32[2048,256]{1,0:T(8,128)}, u32[]{:S(2)}, u32[]{:S(2)}) collective-permute-start(f32[2048,256]{1,0:T(8,128)} %get-tuple-element.25.own), channel_id=1, source_target_pairs={{0,2},{3,1},{4,6},{7,5},{8,10},{11,9},{12,14},{15,13},{16,18},{19,... | collective-permute-start | bytes 6291464 | tf_op jit(solution)/shard_map/ppermute | solution.py:444
  285.8 115.3 %collective-permute-start.11 = (f32[2,2048,256]{2,1,0:T(8,128)}, f32[2,2048,256]{2,1,0:T(8,128)}, u32[]{:S(2)}, u32[]{:S(2)}) collective-permute-start(f32[2,2048,256]{2,1,0:T(8,128)} %get-tuple-element.17), channel_id=1, source_target_pairs={{1,0},{2,3},{5,4},{6,7},{9,8},{10,11},{13,12},{14,15},{17,16},{18,... | collective-permute-start | bytes 12582920 | tf_op jit(solution)/shard_map/ppermute | solution.py:446
  311.1 99.9 %collective-permute-start = (f32[2048,256]{1,0:T(8,128)}, f32[2048,256]{1,0:T(8,128)}, u32[]{:S(2)}, u32[]{:S(2)}) collective-permute-start(f32[2048,256]{1,0:T(8,128)} %get-tuple-element.26.own), channel_id=1, source_target_pairs={{1,2},{2,1},{5,6},{6,5},{9,10},{10,9},{13,14},{14,13},{17,18},{18,... | collective-permute-start | bytes 6291464 | tf_op jit(solution)/shard_map/ppermute | solution.py:443
  314.7 96.3 %collective-permute-start.1 = (f32[2048,256]{1,0:T(8,128)}, f32[2048,256]{1,0:T(8,128)}, u32[]{:S(2)}, u32[]{:S(2)}) collective-permute-start(f32[2048,256]{1,0:T(8,128)} %get-tuple-element.26.own), channel_id=1, source_target_pairs={{0,1},{3,2},{4,5},{7,6},{8,9},{11,10},{12,13},{15,14},{16,17},{19,... | collective-permute-start | bytes 6291464 | tf_op jit(solution)/shard_map/ppermute | solution.py:442
  319.2 108.8 %collective-permute-start.2 = (f32[2048,256]{1,0:T(8,128)}, f32[2048,256]{1,0:T(8,128)}, u32[]{:S(2)}, u32[]{:S(2)}) collective-permute-start(f32[2048,256]{1,0:T(8,128)} %get-tuple-element.26.own), channel_id=1, source_target_pairs={{0,2},{3,1},{4,6},{7,5},{8,10},{11,9},{12,14},{15,13},{16,18},{19,... | collective-permute-start | bytes 6291464 | tf_op jit(solution)/shard_map/ppermute | solution.py:444
  321.8 84.4 %all-to-all-start.4 = ((f32[8,2,256,128]{3,2,1,0:T(8,128)}), f32[8,2,256,128]{3,2,1,0:T(8,128)}, u32[]{:S(2)}, u32[]{:S(2)}) async-start(f32[8,2,256,128]{3,2,1,0:T(8,128)} %bitcast.40), calls=%async_computation.4 | async-start | bytes 4194304 | tf_op jit(solution)/shard_map/all_to_all | solution.py:449
  366.4 124.6 %collective-permute-start.7 = (f32[2,2048,256]{2,1,0:T(8,128)}, f32[2,2048,256]{2,1,0:T(8,128)}, u32[]{:S(2)}, u32[]{:S(2)}) collective-permute-start(f32[2,2048,256]{2,1,0:T(8,128)} %get-tuple-element.15), channel_id=1, source_target_pairs={{1,0},{2,3},{5,4},{6,7},{9,8},{10,11},{13,12},{14,15},{17,16},{18,... | collective-permute-start | bytes 12582920 | tf_op jit(solution)/shard_map/ppermute | solution.py:446
  406.2 89.9 %all-to-all-start.2 = ((f32[8,2,256,256]{3,2,1,0:T(8,128)}), f32[8,2,256,256]{3,2,1,0:T(8,128)}, u32[]{:S(2)}, u32[]{:S(2)}) async-start(f32[8,2,256,256]{3,2,1,0:T(8,128)} %bitcast.47), calls=%async_computation.2 | async-start | bytes 8388608 | tf_op jit(solution)/shard_map/all_to_all | solution.py:449
  451.9 128.6 %collective-permute-start.3 = (f32[2,2048,256]{2,1,0:T(8,128)}, f32[2,2048,256]{2,1,0:T(8,128)}, u32[]{:S(2)}, u32[]{:S(2)}) collective-permute-start(f32[2,2048,256]{2,1,0:T(8,128)} %get-tuple-element.13), channel_id=1, source_target_pairs={{1,0},{2,3},{5,4},{6,7},{9,8},{10,11},{13,12},{14,15},{17,16},{18,... | collective-permute-start | bytes 12582920 | tf_op jit(solution)/shard_map/ppermute | solution.py:446
  496.2 89.5 %all-to-all-start.1 = ((f32[8,2,256,256]{3,2,1,0:T(8,128)}), f32[8,2,256,256]{3,2,1,0:T(8,128)}, u32[]{:S(2)}, u32[]{:S(2)}) async-start(f32[8,2,256,256]{3,2,1,0:T(8,128)} %bitcast.49), calls=%async_computation.1 | async-start | bytes 8388608 | tf_op jit(solution)/shard_map/all_to_all | solution.py:449
  585.6 53.7 %all-to-all-start = ((f32[8,2,256,256]{3,2,1,0:T(8,128)}), f32[8,2,256,256]{3,2,1,0:T(8,128)}, u32[]{:S(2)}, u32[]{:S(2)}) async-start(f32[8,2,256,256]{3,2,1,0:T(8,128)} %bitcast.48), calls=%async_computation | async-start | bytes 8388608 | tf_op jit(solution)/shard_map/all_to_all | solution.py:449
  670.2 53.7 %all-to-all-start.8 = ((f32[8,2,64,1024]{3,2,1,0:T(8,128)}), f32[8,2,64,1024]{3,2,1,0:T(8,128)}, u32[]{:S(2)}, u32[]{:S(2)}) async-start(f32[8,2,64,1024]{3,2,1,0:T(8,128)} %copy.25), calls=%async_computation.8 | async-start | bytes 8388608 | tf_op jit(solution)/shard_map/all_to_all | solution.py:459
  723.9 53.7 %all-to-all-start.7 = ((f32[8,2,64,1024]{3,2,1,0:T(8,128)}), f32[8,2,64,1024]{3,2,1,0:T(8,128)}, u32[]{:S(2)}, u32[]{:S(2)}) async-start(f32[8,2,64,1024]{3,2,1,0:T(8,128)} %copy.22), calls=%async_computation.7 | async-start | bytes 8388608 | tf_op jit(solution)/shard_map/all_to_all | solution.py:459
  831.3 53.7 %all-to-all-start.5 = ((f32[8,2,64,1024]{3,2,1,0:T(8,128)}), f32[8,2,64,1024]{3,2,1,0:T(8,128)}, u32[]{:S(2)}, u32[]{:S(2)}) async-start(f32[8,2,64,1024]{3,2,1,0:T(8,128)} %copy.16), calls=%async_computation.5 | async-start | bytes 8388608 | tf_op jit(solution)/shard_map/all_to_all | solution.py:459
  (18 other events, 1070.4 us)

commit v3 on v2

--- a/solution.py
+++ b/solution.py
@@ -435,13 +435,17 @@
     tables = rows_tables(place, length, blocks)
     chunk = columns // RADIX
     parts = []
+    arrived = []
     begin = 0
     for size in [chunk] * (width // chunk - 1) + [chunk // 2] * 2:
         own = density[:, begin : begin + size]
         begin += size
+        if len(arrived) > 1:
+            own = lax.optimization_barrier((own,) + arrived[-2])[0]
         end = lax.ppermute(own, "gy", [(0, 1), (3, 2)])
         near = lax.ppermute(own, "gy", [(1, 2), (2, 1)])
         far = lax.ppermute(own, "gy", [(0, 2), (3, 1)])
+        arrived.append((near, far))
         kept, sent = rows_stage(flag, own, near, end, far, tables)
         given = lax.ppermute(sent, "gy", [(1, 0), (2, 3)])
         mine = jnp.where(inner, kept, given)

time: 902 us -> 1040 us (1.15)
  starting transfers between devices: 158 us -> 308 us
    ppermute x5, starting transfers between devices: 86.4 us -> 176 us  [line_transform(): end = lax.ppermute(own, 'gy', [(0, 1), (3, 2)])]
    ppermute x5, starting transfers between devices: 16.2 us -> 77.7 us  [line_transform(): far = lax.ppermute(own, 'gy', [(0, 2), (3, 1)])]
    ppermute x5, waiting for transfers between devices: 51.1 us -> 73.6 us  [line_transform(): far = lax.ppermute(own, 'gy', [(0, 2), (3, 1)])]
    ppermute x5, waiting for transfers between devices: 50.8 us -> 31.3 us  [line_transform(): end = lax.ppermute(own, 'gy', [(0, 1), (3, 2)])]
    ppermute x5, waiting for transfers between devices: 203 us -> 191 us  [line_transform(): given = lax.ppermute(sent, 'gy', [(1, 0), (2, 3)])]
  transfers between devices with their start and end apart: 29 -> 29, of which waited for: 14 -> 14; matrix products, arithmetic and copies ran while one was open for 10% -> 9% of each run, Pallas kernels for 16% -> 14%
where the time goes in v3:
time: 1040 us
  waiting for transfers between devices  445 us (43%)
  starting transfers between devices  308 us (30%)
  Pallas kernels  165 us (16%)
  local copies, waits for them, and re-layouts  103 us (10%)
  other arithmetic  15.3 us (1%)
    ppermute x5, waiting for transfers between devices, line_transform(): given = lax.ppermute(sent, 'gy', [(1, 0), (2, 3)])  191 us
    ppermute x5, starting transfers between devices, line_transform(): end = lax.ppermute(own, 'gy', [(0, 1), (3, 2)])  176 us
    pallas_call x5, Pallas kernels, rows_stage(): pl.pallas_call(rows_kernel, out_shape=(shape, shape), in_specs=[pl.BlockS...  108 us
    all_to_all x4, waiting for transfers between devices, line_transform(): lax.all_to_all(result, 'gx', split_axis=0, concat_axis=0, tiled=True)  103 us
    ppermute x5, starting transfers between devices, line_transform(): far = lax.ppermute(own, 'gy', [(0, 2), (3, 1)])  77.7 us
    ppermute x5, waiting for transfers between devices, line_transform(): far = lax.ppermute(own, 'gy', [(0, 2), (3, 1)])  73.6 us
    all_to_all x5, waiting for transfers between devices, line_transform(): lax.all_to_all(mine, 'gx', split_axis=0, concat_axis=0, tiled=True)  45.2 us
    pallas_call x4, Pallas kernels, columns_stage(): pl.pallas_call(columns_kernel, grid=(1,), out_shape=jax.ShapeDtypeStruct(...  43.9 us
  transfers between devices with their start and end apart: 29, of which 14 were waited for; matrix products, arithmetic and copies ran while one was open for 9% of the time, Pallas kernels for 14%

profile of v3, /device:TPU:0, one launch (start us, length us, event | category | flops | bytes accessed | tf_op | source)
XLA Modules:
  0.0 1037.4 jit_solution(6393908409735241373)
XLA Ops:
  24.5 35.9 %collective-permute-done.6.far = f32[2048,256]{1,0:T(8,128)} collective-permute-done((f32[2048,256]{1,0:T(8,128)S(1)}, f32[2048,256]{1,0:T(8,128)}, u32[]{:S(2)}, u32[]{:S(2)}) %collective-permute-start.6) | collective-permute-done | bytes 2097184 | tf_op jit(solution)/shard_map/ppermute | solution.py:447
  61.1 93.8 %collective-permute-start.13 = (f32[2048,128]{1,0:T(8,128)S(1)}, f32[2048,128]{1,0:T(8,128)S(1)}, u32[]{:S(2)}, u32[]{:S(2)}) collective-permute-start(f32[2048,128]{1,0:T(8,128)S(1)} %get-tuple-element.22.own), channel_id=1, source_target_pairs={{0,1},{3,2},{4,5},{7,6},{8,9},{11,10},{12,13},{15,14},{16,17},{19,... | collective-permute-start | bytes 3145736 | tf_op jit(solution)/shard_map/ppermute | solution.py:445
  159.9 63.5 %collective-permute-start.10 = (f32[2048,256]{1,0:T(8,128)}, f32[2048,256]{1,0:T(8,128)}, u32[]{:S(2)}, u32[]{:S(2)}) collective-permute-start(f32[2048,256]{1,0:T(8,128)} %get-tuple-element.19.own), channel_id=1, source_target_pairs={{0,2},{3,1},{4,6},{7,5},{8,10},{11,9},{12,14},{15,13},{16,18},{19,... | collective-permute-start | bytes 6291464 | tf_op jit(solution)/shard_map/ppermute | solution.py:447
  227.9 18.0 %shard_map.53 = (f32[2,2048,128]{2,1,0:T(8,128)}, f32[2,2048,128]{2,1,0:T(8,128)}) custom-call(s32[1]{0:T(128)} %bitcast.flag, f32[2048,128]{1,0:T(8,128)} %copy-done.6, f32[2048,128]{1,0:T(8,128)} %copy-done.8, f32[2048,128]{1,0:T(8,128)} %copy-done.9, f32[2048,128]{1,0:T(8,128)} %copy-done.10, f32[17,256,128]{2,1,0:T(8,128)} %broadcast_in_dim.24.cosine, ...), custom_call_target="tpu_custom_call" | custom-call | flops 30000001024 | bytes 25165824 | tf_op jit(solution)/shard_map/pallas_call | solution.py:282
  247.2 17.9 %collective-permute-done.10.far = f32[2048,256]{1,0:T(8,128)} collective-permute-done((f32[2048,256]{1,0:T(8,128)}, f32[2048,256]{1,0:T(8,128)}, u32[]{:S(2)}, u32[]{:S(2)}) %collective-permute-start.10) | collective-permute-done | bytes 2097184 | tf_op jit(solution)/shard_map/ppermute | solution.py:447
  265.8 68.6 %collective-permute-start.17 = (f32[2048,128]{1,0:T(8,128)}, f32[2048,128]{1,0:T(8,128)}, u32[]{:S(2)}, u32[]{:S(2)}) collective-permute-start(f32[2048,128]{1,0:T(8,128)} %get-tuple-element.25.own), channel_id=1, source_target_pairs={{0,1},{3,2},{4,5},{7,6},{8,9},{11,10},{12,13},{15,14},{16,17},{19,... | collective-permute-start | bytes 3145736 | tf_op jit(solution)/shard_map/ppermute | solution.py:445
  339.3 12.4 %collective-permute-done.15 = f32[2,2048,128]{2,1,0:T(8,128)S(1)} collective-permute-done((f32[2,2048,128]{2,1,0:T(8,128)}, f32[2,2048,128]{2,1,0:T(8,128)S(1)}, u32[]{:S(2)}, u32[]{:S(2)}) %collective-permute-start.15) | collective-permute-done | bytes 2097184 | tf_op jit(solution)/shard_map/ppermute | solution.py:450
  360.1 19.8 %collective-permute-done.18.far = f32[2048,128]{1,0:T(8,128)} collective-permute-done((f32[2048,128]{1,0:T(8,128)}, f32[2048,128]{1,0:T(8,128)}, u32[]{:S(2)}, u32[]{:S(2)}) %collective-permute-start.18) | collective-permute-done | bytes 1048608 | tf_op jit(solution)/shard_map/ppermute | solution.py:447
  379.9 18.0 %shard_map.54 = (f32[2,2048,128]{2,1,0:T(8,128)}, f32[2,2048,128]{2,1,0:T(8,128)}) custom-call(s32[1]{0:T(128)} %bitcast.flag, f32[2048,128]{1,0:T(8,128)} %get-tuple-element.25.own, f32[2048,128]{1,0:T(8,128)} %copy-done.11, f32[2048,128]{1,0:T(8,128)} %collective-permute-done.17.end, f32[2048,128]{1,0:T(8,128)} %collective-permute-done.18.far, ...), custom_call_target="tpu_custom_call" | custom-call | flops 30000001024 | bytes 25165824 | tf_op jit(solution)/shard_map/pallas_call | solution.py:282
  399.3 25.5 %collective-permute-done.1.end = f32[2048,256]{1,0:T(8,128)} collective-permute-done((f32[2048,256]{1,0:T(8,128)}, f32[2048,256]{1,0:T(8,128)}, u32[]{:S(2)}, u32[]{:S(2)}) %collective-permute-start.1) | collective-permute-done | bytes 2097184 | tf_op jit(solution)/shard_map/ppermute | solution.py:445
  424.8 23.9 %shard_map.50 = (f32[2,2048,256]{2,1,0:T(8,128)}, f32[2,2048,256]{2,1,0:T(8,128)}) custom-call(s32[1]{0:T(128)} %bitcast.flag, f32[2048,256]{1,0:T(8,128)} %get-tuple-element.32.own, f32[2048,256]{1,0:T(8,128)} %collective-permute-done.near, f32[2048,256]{1,0:T(8,128)} %collective-permute-done.1.end, f32[2048,256]{1,0:T(8,128)} %collective-permute-done.2.far, ...), custom_call_target="tpu_custom_call" | custom-call | flops 30000001024 | bytes 25165824 | tf_op jit(solution)/shard_map/pallas_call | solution.py:282
  469.7 23.8 %shard_map.51 = (f32[2,2048,256]{2,1,0:T(8,128)}, f32[2,2048,256]{2,1,0:T(8,128)}) custom-call(s32[1]{0:T(128)} %bitcast.flag, f32[2048,256]{1,0:T(8,128)} %copy-done.5, f32[2048,256]{1,0:T(8,128)} %collective-permute-done.4.near, f32[2048,256]{1,0:T(8,128)} %collective-permute-done.5.end, f32[2048,256]{1,0:T(8,128)} %collective-permute-done.6.far, ...), custom_call_target="tpu_custom_call" | custom-call | flops 30000001024 | bytes 25165824 | tf_op jit(solution)/shard_map/pallas_call | solution.py:282
  494.8 49.6 %collective-permute-done.3 = f32[2,2048,256]{2,1,0:T(8,128)} collective-permute-done((f32[2,2048,256]{2,1,0:T(8,128)}, f32[2,2048,256]{2,1,0:T(8,128)}, u32[]{:S(2)}, u32[]{:S(2)}) %collective-permute-start.3) | collective-permute-done | bytes 4194336 | tf_op jit(solution)/shard_map/ppermute | solution.py:450
  554.4 24.0 %shard_map.52 = (f32[2,2048,256]{2,1,0:T(8,128)}, f32[2,2048,256]{2,1,0:T(8,128)}) custom-call(s32[1]{0:T(128)} %bitcast.flag, f32[2048,256]{1,0:T(8,128)} %get-tuple-element.19.own, f32[2048,256]{1,0:T(8,128)} %collective-permute-done.8.near, f32[2048,256]{1,0:T(8,128)} %collective-permute-done.9.end, f32[2048,256]{1,0:T(8,128)} %collective-permute-done.10.far, ...), custom_call_target="tpu_custom_call" | custom-call | flops 30000001024 | bytes 25165824 | tf_op jit(solution)/shard_map/pallas_call | solution.py:282
  579.6 54.7 %collective-permute-done.7 = f32[2,2048,256]{2,1,0:T(8,128)} collective-permute-done((f32[2,2048,256]{2,1,0:T(8,128)}, f32[2,2048,256]{2,1,0:T(8,128)}, u32[]{:S(2)}, u32[]{:S(2)}) %collective-permute-start.7) | collective-permute-done | bytes 4194336 | tf_op jit(solution)/shard_map/ppermute | solution.py:450
  644.0 74.6 %collective-permute-done.11 = f32[2,2048,256]{2,1,0:T(8,128)} collective-permute-done((f32[2,2048,256]{2,1,0:T(8,128)}, f32[2,2048,256]{2,1,0:T(8,128)}, u32[]{:S(2)}, u32[]{:S(2)}) %collective-permute-start.11) | collective-permute-done | bytes 4194336 | tf_op jit(solution)/shard_map/ppermute | solution.py:450
  732.4 45.2 %all-to-all-done.2.refs_2_ = f32[8,2,256,256]{3,2,1,0:T(8,128)} async-done(((f32[8,2,256,256]{3,2,1,0:T(8,128)}), f32[8,2,256,256]{3,2,1,0:T(8,128)}, u32[]{:S(2)}, u32[]{:S(2)}) %all-to-all-start.2) | async-done | bytes 4194336 | tf_op jit(solution)/shard_map/all_to_all | solution.py:453
  813.3 11.0 %shard_map.56 = f32[2,2048,256]{2,1,0:T(8,128)} custom-call(f32[8,2,256,256]{3,2,1,0:T(8,128)} %all-to-all-done.refs_0_, f32[8,2,256,256]{3,2,1,0:T(8,128)} %all-to-all-done.1.refs_1_, f32[8,2,256,256]{3,2,1,0:T(8,128)} %all-to-all-done.2.refs_2_, f32[8,2,256,128]{3,2,1,0:T(8,128)} %copy-done.4, f32[8,2,256,128]{3,2,1,0:T(8,128)} %all-to-all-done.4.refs_4_, ...), custom_call_target="tpu_custom_call" | custom-call | flops 8000000000 | bytes 8388608 | tf_op jit(solution)/shard_map/pallas_call | solution.py:375
  844.2 17.9 %all-to-all-done.5.refs_0_ = f32[8,2,64,1024]{3,2,1,0:T(8,128)} async-done(((f32[8,2,64,1024]{3,2,1,0:T(8,128)}), f32[8,2,64,1024]{3,2,1,0:T(8,128)}, u32[]{:S(2)}, u32[]{:S(2)}) %all-to-all-start.5) | async-done | bytes 4194336 | tf_op jit(solution)/shard_map/all_to_all | solution.py:463
  897.6 18.2 %all-to-all-done.6.refs_1_ = f32[8,2,64,1024]{3,2,1,0:T(8,128)} async-done(((f32[8,2,64,1024]{3,2,1,0:T(8,128)}), f32[8,2,64,1024]{3,2,1,0:T(8,128)}, u32[]{:S(2)}, u32[]{:S(2)}) %all-to-all-start.6) | async-done | bytes 4194336 | tf_op jit(solution)/shard_map/all_to_all | solution.py:463
  920.4 11.0 %shard_map.58 = f32[2,2048,256]{2,1,0:T(8,128)} custom-call(f32[8,2,256,256]{3,2,1,0:T(8,128)} %all-to-all-done.refs_0_, f32[8,2,256,256]{3,2,1,0:T(8,128)} %all-to-all-done.1.refs_1_, f32[8,2,256,256]{3,2,1,0:T(8,128)} %all-to-all-done.2.refs_2_, f32[8,2,256,128]{3,2,1,0:T(8,128)} %copy-done.4, f32[8,2,256,128]{3,2,1,0:T(8,128)} %all-to-all-done.4.refs_4_, ...), custom_call_target="tpu_custom_call" | custom-call | flops 8000000000 | bytes 8388608 | tf_op jit(solution)/shard_map/pallas_call | solution.py:375
  951.4 18.1 %all-to-all-done.7.refs_2_ = f32[8,2,64,1024]{3,2,1,0:T(8,128)} async-done(((f32[8,2,64,1024]{3,2,1,0:T(8,128)}), f32[8,2,64,1024]{3,2,1,0:T(8,128)}, u32[]{:S(2)}, u32[]{:S(2)}) %all-to-all-start.7) | async-done | bytes 4194336 | tf_op jit(solution)/shard_map/all_to_all | solution.py:463
  974.1 49.1 %all-to-all-done.8.refs_3_ = f32[8,2,64,1024]{3,2,1,0:T(8,128)} async-done(((f32[8,2,64,1024]{3,2,1,0:T(8,128)}), f32[8,2,64,1024]{3,2,1,0:T(8,128)}, u32[]{:S(2)}, u32[]{:S(2)}) %all-to-all-start.8) | async-done | bytes 4194336 | tf_op jit(solution)/shard_map/all_to_all | solution.py:463
  1023.5 13.9 %shard_map.59 = (f32[2048,1024]{1,0:T(8,128)}, f32[2048,1024]{1,0:T(8,128)}) custom-call(f32[8,2,64,1024]{3,2,1,0:T(8,128)} %all-to-all-done.5.refs_0_, f32[8,2,64,1024]{3,2,1,0:T(8,128)} %all-to-all-done.6.refs_1_, f32[8,2,64,1024]{3,2,1,0:T(8,128)} %all-to-all-done.7.refs_2_, f32[8,2,64,1024]{3,2,1,0:T(8,128)} %all-to-all-done.8.refs_3_, ...), custom_call_target="tpu_custom_call" | custom-call | tf_op jit(solution)/shard_map/pallas_call | solution.py:416
  (117 shorter events, 228.0 us)
Async XLA Ops:
  15.7 142.3 %collective-permute-start = (f32[2048,256]{1,0:T(8,128)}, f32[2048,256]{1,0:T(8,128)}, u32[]{:S(2)}, u32[]{:S(2)}) collective-permute-start(f32[2048,256]{1,0:T(8,128)} %get-tuple-element.32.own), channel_id=1, source_target_pairs={{1,2},{2,1},{5,6},{6,5},{9,10},{10,9},{13,14},{14,13},{17,18},{18,... | collective-permute-start | bytes 6291464 | tf_op jit(solution)/shard_map/ppermute | solution.py:446
  17.7 140.3 %collective-permute-start.2 = (f32[2048,256]{1,0:T(8,128)}, f32[2048,256]{1,0:T(8,128)}, u32[]{:S(2)}, u32[]{:S(2)}) collective-permute-start(f32[2048,256]{1,0:T(8,128)} %get-tuple-element.32.own), channel_id=1, source_target_pairs={{0,2},{3,1},{4,6},{7,5},{8,10},{11,9},{12,14},{15,13},{16,18},{19,... | collective-permute-start | bytes 6291464 | tf_op jit(solution)/shard_map/ppermute | solution.py:447
  60.4 163.0 %collective-permute-start.12 = (f32[2048,128]{1,0:T(8,128)S(1)}, f32[2048,128]{1,0:T(8,128)S(1)}, u32[]{:S(2)}, u32[]{:S(2)}) collective-permute-start(f32[2048,128]{1,0:T(8,128)S(1)} %get-tuple-element.22.own), channel_id=1, source_target_pairs={{1,2},{2,1},{5,6},{6,5},{9,10},{10,9},{13,14},{14,13},{17,18},{18,... | collective-permute-start | bytes 3145736 | tf_op jit(solution)/shard_map/ppermute | solution.py:446
  61.1 162.3 %collective-permute-start.13 = (f32[2048,128]{1,0:T(8,128)S(1)}, f32[2048,128]{1,0:T(8,128)S(1)}, u32[]{:S(2)}, u32[]{:S(2)}) collective-permute-start(f32[2048,128]{1,0:T(8,128)S(1)} %get-tuple-element.22.own), channel_id=1, source_target_pairs={{0,1},{3,2},{4,5},{7,6},{8,9},{11,10},{12,13},{15,14},{16,17},{19,... | collective-permute-start | bytes 3145736 | tf_op jit(solution)/shard_map/ppermute | solution.py:445
  154.9 68.5 %collective-permute-start.14 = (f32[2048,128]{1,0:T(8,128)S(1)}, f32[2048,128]{1,0:T(8,128)S(1)}, u32[]{:S(2)}, u32[]{:S(2)}) collective-permute-start(f32[2048,128]{1,0:T(8,128)S(1)} %get-tuple-element.22.own), channel_id=1, source_target_pairs={{0,2},{3,1},{4,6},{7,5},{8,10},{11,9},{12,14},{15,13},{16,18},{19,... | collective-permute-start | bytes 3145736 | tf_op jit(solution)/shard_map/ppermute | solution.py:447
  158.0 89.2 %collective-permute-start.8 = (f32[2048,256]{1,0:T(8,128)}, f32[2048,256]{1,0:T(8,128)}, u32[]{:S(2)}, u32[]{:S(2)}) collective-permute-start(f32[2048,256]{1,0:T(8,128)} %get-tuple-element.19.own), channel_id=1, source_target_pairs={{1,2},{2,1},{5,6},{6,5},{9,10},{10,9},{13,14},{14,13},{17,18},{18,... | collective-permute-start | bytes 6291464 | tf_op jit(solution)/shard_map/ppermute | solution.py:446
  159.9 105.1 %collective-permute-start.10 = (f32[2048,256]{1,0:T(8,128)}, f32[2048,256]{1,0:T(8,128)}, u32[]{:S(2)}, u32[]{:S(2)}) collective-permute-start(f32[2048,256]{1,0:T(8,128)} %get-tuple-element.19.own), channel_id=1, source_target_pairs={{0,2},{3,1},{4,6},{7,5},{8,10},{11,9},{12,14},{15,13},{16,18},{19,... | collective-permute-start | bytes 6291464 | tf_op jit(solution)/shard_map/ppermute | solution.py:447
  245.9 105.8 %collective-permute-start.15 = (f32[2,2048,128]{2,1,0:T(8,128)}, f32[2,2048,128]{2,1,0:T(8,128)S(1)}, u32[]{:S(2)}, u32[]{:S(2)}) collective-permute-start(f32[2,2048,128]{2,1,0:T(8,128)} %get-tuple-element.24), channel_id=1, source_target_pairs={{1,0},{2,3},{5,4},{6,7},{9,8},{10,11},{13,12},{14,15},{17,16},{18,... | collective-permute-start | bytes 6291464 | tf_op jit(solution)/shard_map/ppermute | solution.py:450
  265.1 95.0 %collective-permute-start.16 = (f32[2048,128]{1,0:T(8,128)}, f32[2048,128]{1,0:T(8,128)S(1)}, u32[]{:S(2)}, u32[]{:S(2)}) collective-permute-start(f32[2048,128]{1,0:T(8,128)} %get-tuple-element.25.own), channel_id=1, source_target_pairs={{1,2},{2,1},{5,6},{6,5},{9,10},{10,9},{13,14},{14,13},{17,18},{18,... | collective-permute-start | bytes 3145736 | tf_op jit(solution)/shard_map/ppermute | solution.py:446
  265.8 94.2 %collective-permute-start.17 = (f32[2048,128]{1,0:T(8,128)}, f32[2048,128]{1,0:T(8,128)}, u32[]{:S(2)}, u32[]{:S(2)}) collective-permute-start(f32[2048,128]{1,0:T(8,128)} %get-tuple-element.25.own), channel_id=1, source_target_pairs={{0,1},{3,2},{4,5},{7,6},{8,9},{11,10},{12,13},{15,14},{16,17},{19,... | collective-permute-start | bytes 3145736 | tf_op jit(solution)/shard_map/ppermute | solution.py:445
  336.8 88.1 %collective-permute-start.1 = (f32[2048,256]{1,0:T(8,128)}, f32[2048,256]{1,0:T(8,128)}, u32[]{:S(2)}, u32[]{:S(2)}) collective-permute-start(f32[2048,256]{1,0:T(8,128)} %get-tuple-element.32.own), channel_id=1, source_target_pairs={{0,1},{3,2},{4,5},{7,6},{8,9},{11,10},{12,13},{15,14},{16,17},{19,... | collective-permute-start | bytes 6291464 | tf_op jit(solution)/shard_map/ppermute | solution.py:445
  351.7 118.0 %collective-permute-start.5 = (f32[2048,256]{1,0:T(8,128)}, f32[2048,256]{1,0:T(8,128)}, u32[]{:S(2)}, u32[]{:S(2)}) collective-permute-start(f32[2048,256]{1,0:T(8,128)} %copy-done.5), channel_id=1, source_target_pairs={{0,1},{3,2},{4,5},{7,6},{8,9},{11,10},{12,13},{15,14},{16,17},{19,... | collective-permute-start | bytes 6291464 | tf_op jit(solution)/shard_map/ppermute | solution.py:445
  356.3 103.3 %all-to-all-start.3 = ((f32[8,2,256,128]{3,2,1,0:T(8,128)}), f32[8,2,256,128]{3,2,1,0:T(8,128)S(1)}, u32[]{:S(2)}, u32[]{:S(2)}) async-start(f32[8,2,256,128]{3,2,1,0:T(8,128)} %bitcast.41), calls=%async_computation.3 | async-start | bytes 4194304 | tf_op jit(solution)/shard_map/all_to_all | solution.py:453
  397.9 60.0 %collective-permute-start.19 = (f32[2,2048,128]{2,1,0:T(8,128)}, f32[2,2048,128]{2,1,0:T(8,128)S(1)}, u32[]{:S(2)}, u32[]{:S(2)}) collective-permute-start(f32[2,2048,128]{2,1,0:T(8,128)} %get-tuple-element.27), channel_id=1, source_target_pairs={{1,0},{2,3},{5,4},{6,7},{9,8},{10,11},{13,12},{14,15},{17,16},{18,... | collective-permute-start | bytes 6291464 | tf_op jit(solution)/shard_map/ppermute | solution.py:450
  448.7 95.7 %collective-permute-start.3 = (f32[2,2048,256]{2,1,0:T(8,128)}, f32[2,2048,256]{2,1,0:T(8,128)}, u32[]{:S(2)}, u32[]{:S(2)}) collective-permute-start(f32[2,2048,256]{2,1,0:T(8,128)} %get-tuple-element.16), channel_id=1, source_target_pairs={{1,0},{2,3},{5,4},{6,7},{9,8},{10,11},{13,12},{14,15},{17,16},{18,... | collective-permute-start | bytes 12582920 | tf_op jit(solution)/shard_map/ppermute | solution.py:450
  450.0 104.4 %collective-permute-start.9 = (f32[2048,256]{1,0:T(8,128)}, f32[2048,256]{1,0:T(8,128)}, u32[]{:S(2)}, u32[]{:S(2)}) collective-permute-start(f32[2048,256]{1,0:T(8,128)} %get-tuple-element.19.own), channel_id=1, source_target_pairs={{0,1},{3,2},{4,5},{7,6},{8,9},{11,10},{12,13},{15,14},{16,17},{19,... | collective-permute-start | bytes 6291464 | tf_op jit(solution)/shard_map/ppermute | solution.py:445
  459.6 90.0 %all-to-all-start.4 = ((f32[8,2,256,128]{3,2,1,0:T(8,128)}), f32[8,2,256,128]{3,2,1,0:T(8,128)}, u32[]{:S(2)}, u32[]{:S(2)}) async-start(f32[8,2,256,128]{3,2,1,0:T(8,128)} %bitcast.40), calls=%async_computation.4 | async-start | bytes 4194304 | tf_op jit(solution)/shard_map/all_to_all | solution.py:453
  493.6 140.7 %collective-permute-start.7 = (f32[2,2048,256]{2,1,0:T(8,128)}, f32[2,2048,256]{2,1,0:T(8,128)}, u32[]{:S(2)}, u32[]{:S(2)}) collective-permute-start(f32[2,2048,256]{2,1,0:T(8,128)} %get-tuple-element.18), channel_id=1, source_target_pairs={{1,0},{2,3},{5,4},{6,7},{9,8},{10,11},{13,12},{14,15},{17,16},{18,... | collective-permute-start | bytes 12582920 | tf_op jit(solution)/shard_map/ppermute | solution.py:450
  549.6 89.9 %all-to-all-start = ((f32[8,2,256,256]{3,2,1,0:T(8,128)}), f32[8,2,256,256]{3,2,1,0:T(8,128)}, u32[]{:S(2)}, u32[]{:S(2)}) async-start(f32[8,2,256,256]{3,2,1,0:T(8,128)} %bitcast.47), calls=%async_computation | async-start | bytes 8388608 | tf_op jit(solution)/shard_map/all_to_all | solution.py:453
  578.3 140.3 %collective-permute-start.11 = (f32[2,2048,256]{2,1,0:T(8,128)}, f32[2,2048,256]{2,1,0:T(8,128)}, u32[]{:S(2)}, u32[]{:S(2)}) collective-permute-start(f32[2,2048,256]{2,1,0:T(8,128)} %get-tuple-element.21), channel_id=1, source_target_pairs={{1,0},{2,3},{5,4},{6,7},{9,8},{10,11},{13,12},{14,15},{17,16},{18,... | collective-permute-start | bytes 12582920 | tf_op jit(solution)/shard_map/ppermute | solution.py:450
  639.5 84.4 %all-to-all-start.1 = ((f32[8,2,256,256]{3,2,1,0:T(8,128)}), f32[8,2,256,256]{3,2,1,0:T(8,128)}, u32[]{:S(2)}, u32[]{:S(2)}) async-start(f32[8,2,256,256]{3,2,1,0:T(8,128)} %bitcast.49), calls=%async_computation.1 | async-start | bytes 8388608 | tf_op jit(solution)/shard_map/all_to_all | solution.py:453
  723.9 53.7 %all-to-all-start.2 = ((f32[8,2,256,256]{3,2,1,0:T(8,128)}), f32[8,2,256,256]{3,2,1,0:T(8,128)}, u32[]{:S(2)}, u32[]{:S(2)}) async-start(f32[8,2,256,256]{3,2,1,0:T(8,128)} %bitcast.48), calls=%async_computation.2 | async-start | bytes 8388608 | tf_op jit(solution)/shard_map/all_to_all | solution.py:453
  808.5 53.7 %all-to-all-start.5 = ((f32[8,2,64,1024]{3,2,1,0:T(8,128)}), f32[8,2,64,1024]{3,2,1,0:T(8,128)}, u32[]{:S(2)}, u32[]{:S(2)}) async-start(f32[8,2,64,1024]{3,2,1,0:T(8,128)} %copy.16), calls=%async_computation.5 | async-start | bytes 8388608 | tf_op jit(solution)/shard_map/all_to_all | solution.py:463
  915.8 53.7 %all-to-all-start.7 = ((f32[8,2,64,1024]{3,2,1,0:T(8,128)}), f32[8,2,64,1024]{3,2,1,0:T(8,128)}, u32[]{:S(2)}, u32[]{:S(2)}) async-start(f32[8,2,64,1024]{3,2,1,0:T(8,128)} %copy.22), calls=%async_computation.7 | async-start | bytes 8388608 | tf_op jit(solution)/shard_map/all_to_all | solution.py:463
  (17 other events, 961.3 us)
